TPU v7x, 32 devices: a whole 2x2x4 slice. The times are simulated.
32 devices in a mesh: dp: 8 (over z, y), tensor: 4 (over x, core).
Axes of the slice: x: 2, y: 2, z: 4, core: 2. Of those that a mesh axis runs over, the one named last changes fastest.
Arguments:
- layer_input: bfloat16 [4096, 2048], P(('dp', 'tensor')), may hold values from -6 to 6
- doc_lengths: int32 [8, 8], P('dp'), may hold values from 1 to 505, as said below
- w_query: bfloat16 [2048, 2048], P(None, 'tensor'), may hold values from -0.125 to 0.125
- w_key: bfloat16 [2048, 512], P(None, 'tensor'), may hold values from -0.125 to 0.125
- w_value: bfloat16 [2048, 512], P(None, 'tensor'), may hold values from -0.125 to 0.125
- w_out: bfloat16 [2048, 2048], P('tensor'), may hold values from -0.5 to 0.5
- w_gate: bfloat16 [2048, 8192], P(None, 'tensor'), may hold values from -0.125 to 0.125
- w_up: bfloat16 [2048, 8192], P(None, 'tensor'), may hold values from -0.125 to 0.125
- w_down: bfloat16 [8192, 2048], P('tensor'), may hold values from -0.0625 to 0.0625
- gain_attn: float32 [2048], replicated, may hold values from 0.1 to 1.9
- gain_ffn: float32 [2048], replicated, may hold values from 0.1 to 1.9
- gain_query: float32 [64], replicated, may hold values from 0.1 to 1.9
- gain_key: float32 [64], replicated, may hold values from 0.1 to 1.9
- out_grad: bfloat16 [4096, 2048], P(('dp', 'tensor')), may hold values from -6 to 6
Outputs:
- layer_out: bfloat16 [4096, 2048], P(('dp', 'tensor'))
- input_grad: bfloat16 [4096, 2048], P(('dp', 'tensor'))
- grad_query: float32 [2048, 2048], P('dp', 'tensor')
- grad_key: float32 [2048, 512], P('dp', 'tensor')
- grad_value: float32 [2048, 512], P('dp', 'tensor')
- grad_out: float32 [2048, 2048], P('tensor', 'dp')
- grad_gate: float32 [2048, 8192], P('dp', 'tensor')
- grad_up: float32 [2048, 8192], P('dp', 'tensor')
- grad_down: float32 [8192, 2048], P('tensor', 'dp')
- grad_gain_attn: float32 [2048], replicated
- grad_gain_ffn: float32 [2048], replicated
- grad_gain_query: float32 [64], replicated
- grad_gain_key: float32 [64], replicated
Inputs may be any that keep to these rules, and one draw needn't show every extreme that they name: `doc_lengths`: each row's 8 lengths sum to 512. One document of each row, at a place that varies, is longer than 384; each other one has 1 to 16 tokens. In one row all other documents have 1 token.
All inputs are finite; a program needn't handle non-finite values.
Results may differ from a plain program's by a relative error of at most 0.025.
Values may be sent and summed in bfloat16 or wider, within the bound.
A program may use at most 192 MiB of HBM per device.

v0:
```python
import jax
import jax.numpy as jnp
from jax import lax
from jax.sharding import PartitionSpec as P

HEADS = 32
KV = 8


EPSILON = 1e-06
ROPE_BASE = 10000.0
MASKED = -1e30


def norm_gain(row_block, gain_vec):
    factor = lax.rsqrt(jnp.mean(row_block * row_block, axis=-1, keepdims=True) + EPSILON)
    return row_block * factor * gain_vec


def rotate(vector, cosine, sine_table):
    half_width = vector.shape[-1] // 2
    first = vector[..., :half_width]
    second = vector[..., half_width:]
    return jnp.concatenate(
        [first * cosine - second * sine_table, second * cosine + first * sine_table], axis=-1
    )


def head_prep(raw_proj, gain_vec, cosine, sine_table):
    head_width = gain_vec.shape[0]
    per_head = raw_proj.reshape(raw_proj.shape[0], raw_proj.shape[1] // head_width, head_width)
    return rotate(norm_gain(per_head, gain_vec), cosine[:, None, :], sine_table[:, None, :])


def doc_layout(lengths, length):
    doc_ends = jnp.cumsum(lengths)
    places = jnp.arange(length, dtype=jnp.int32)
    passed_end = (places[:, None] >= doc_ends[None, :]).astype(jnp.int32)
    doc_ids = jnp.sum(passed_end, axis=1)
    starts = jnp.sum(passed_end * lengths[None, :], axis=1)
    return (doc_ids, places, places - starts)


def rope_tables(offsets, head_width):
    frequency = ROPE_BASE ** (-jnp.arange(0, head_width, 2, dtype=jnp.float32) / head_width)
    angles = offsets.astype(jnp.float32)[:, None] * frequency[None, :]
    return (jnp.cos(angles), jnp.sin(angles))


def swiglu(gate_proj, up_proj):
    return jax.nn.silu(gate_proj) * up_proj


def matmul_nt(left_mat, right_mat):
    return lax.dot_general(
        left_mat, right_mat, (((1,), (1,)), ((), ())), preferred_element_type=jnp.float32
    )


def matmul_tn(left_mat, right_mat):
    return lax.dot_general(
        left_mat, right_mat, (((0,), (0,)), ((), ())), preferred_element_type=jnp.float32
    )


def per_device(
    layer_input,
    doc_lengths,
    w_query,
    w_key,
    w_value,
    w_out,
    w_gate,
    w_up,
    w_down,
    gain_attn,
    gain_ffn,
    gain_query,
    gain_key,
    out_grad,
):
    tok_rows = layer_input.shape[0]
    head_width = gain_query.shape[0]
    tensor_count = lax.axis_size("tensor")
    length = tok_rows * tensor_count
    per_dev = w_query.shape[1] // head_width
    groups_dev = w_key.shape[1] // head_width
    input_f32 = layer_input.astype(jnp.float32)
    doc_ids, places, offsets = doc_layout(doc_lengths[0], length)
    cosine, sine_table = rope_tables(offsets, head_width)
    attn_in = lax.all_gather(
        norm_gain(input_f32, gain_attn).astype(jnp.bfloat16), "tensor", axis=0, tiled=True
    )
    query_raw = jnp.dot(attn_in, w_query, preferred_element_type=jnp.float32)
    key_raw = jnp.dot(attn_in, w_key, preferred_element_type=jnp.float32).astype(jnp.bfloat16)
    value_raw = jnp.dot(attn_in, w_value, preferred_element_type=jnp.float32).astype(jnp.bfloat16)
    key_f32 = key_raw.astype(jnp.float32)
    queries = head_prep(query_raw, gain_query, cosine, sine_table).astype(jnp.bfloat16)
    key_rot = head_prep(key_f32, gain_key, cosine, sine_table).astype(jnp.bfloat16)
    local_heads = jnp.arange(per_dev, dtype=jnp.int32)
    group_pick = (
        local_heads[:, None] // (HEADS // KV) == jnp.arange(groups_dev, dtype=jnp.int32)[None, :]
    ).astype(jnp.float32)
    pick_low = group_pick.astype(jnp.bfloat16)
    key_heads = jnp.einsum(
        "lgd,hg->lhd", key_rot, pick_low, preferred_element_type=jnp.float32
    ).astype(jnp.bfloat16)
    value_heads = jnp.einsum(
        "lgd,hg->lhd",
        value_raw.reshape(length, groups_dev, head_width),
        pick_low,
        preferred_element_type=jnp.float32,
    ).astype(jnp.bfloat16)
    block_rows = min(512, length)
    block_count = length // block_rows
    score_scale = head_width ** (-0.5)

    def block_scores(block_num):
        row_begin = block_num * block_rows
        query_block = lax.dynamic_slice_in_dim(queries, row_begin, block_rows, 0)
        ids_block = lax.dynamic_slice_in_dim(doc_ids, row_begin, block_rows, 0)
        places_block = lax.dynamic_slice_in_dim(places, row_begin, block_rows, 0)
        scores = (
            jnp.einsum("qhd,khd->hqk", query_block, key_heads, preferred_element_type=jnp.float32)
            * score_scale
        )
        allowed = (ids_block[:, None] == doc_ids[None, :]) & (
            places[None, :] <= places_block[:, None]
        )
        return (query_block, jnp.where(allowed[None], scores, MASKED))

    def forward_block(block_num):
        query_block, scores = block_scores(block_num)
        row_top = jnp.max(scores, axis=-1, keepdims=True)
        exponent = jnp.exp(scores - row_top)
        row_total = jnp.sum(exponent, axis=-1, keepdims=True)
        probabilities = (exponent / row_total).astype(jnp.bfloat16)
        mixed_block = jnp.einsum(
            "hqk,khd->qhd", probabilities, value_heads, preferred_element_type=jnp.float32
        )
        return (mixed_block, row_top + jnp.log(row_total))

    mixed_all, log_totals = lax.map(forward_block, jnp.arange(block_count, dtype=jnp.int32))
    attn_mixed = mixed_all.reshape(length, per_dev * head_width).astype(jnp.bfloat16)
    residual = input_f32 + lax.psum_scatter(
        jnp.dot(attn_mixed, w_out, preferred_element_type=jnp.float32).astype(jnp.bfloat16),
        "tensor",
        scatter_dimension=0,
        tiled=True,
    ).astype(jnp.float32)
    ffn_in = lax.all_gather(
        norm_gain(residual, gain_ffn).astype(jnp.bfloat16), "tensor", axis=0, tiled=True
    )
    gate_proj = jnp.dot(ffn_in, w_gate, preferred_element_type=jnp.float32)
    up_proj = jnp.dot(ffn_in, w_up, preferred_element_type=jnp.float32)
    hidden = swiglu(gate_proj, up_proj).astype(jnp.bfloat16)
    layer_out = (
        residual
        + lax.psum_scatter(
            jnp.dot(hidden, w_down, preferred_element_type=jnp.float32).astype(jnp.bfloat16),
            "tensor",
            scatter_dimension=0,
            tiled=True,
        ).astype(jnp.float32)
    ).astype(jnp.bfloat16)
    grad_rows = lax.all_gather(out_grad, "tensor", axis=0, tiled=True)
    hidden_grad = matmul_nt(grad_rows, w_down)
    grad_down = matmul_tn(hidden, grad_rows)
    unused_value, swiglu_back = jax.vjp(swiglu, gate_proj, up_proj)
    gate_grad, up_grad = swiglu_back(hidden_grad)
    gate_grad = gate_grad.astype(jnp.bfloat16)
    up_grad = up_grad.astype(jnp.bfloat16)
    grad_gate = matmul_tn(ffn_in, gate_grad)
    grad_up = matmul_tn(ffn_in, up_grad)
    ffn_in_grad = lax.psum_scatter(
        (matmul_nt(gate_grad, w_gate) + matmul_nt(up_grad, w_up)).astype(jnp.bfloat16),
        "tensor",
        scatter_dimension=0,
        tiled=True,
    ).astype(jnp.float32)
    unused_norm, ffn_norm_back = jax.vjp(norm_gain, residual, gain_ffn)
    residual_grad, gain_ffn_grad = ffn_norm_back(ffn_in_grad)
    residual_grad = residual_grad + out_grad.astype(jnp.float32)
    res_low = lax.all_gather(residual_grad.astype(jnp.bfloat16), "tensor", axis=0, tiled=True)
    mixed_grad = matmul_nt(res_low, w_out).astype(jnp.bfloat16).reshape(length, per_dev, head_width)
    grad_out = matmul_tn(attn_mixed, res_low)

    def backward_block(running, block_num):
        key_acc, value_acc = running
        query_block, scores = block_scores(block_num)
        probabilities = jnp.exp(scores - log_totals[block_num])
        grad_block = lax.dynamic_slice_in_dim(mixed_grad, block_num * block_rows, block_rows, 0)
        prob_grad = jnp.einsum(
            "qhd,khd->hqk", grad_block, value_heads, preferred_element_type=jnp.float32
        )
        value_acc = value_acc + jnp.einsum(
            "hqk,qhd->khd",
            probabilities.astype(jnp.bfloat16),
            grad_block,
            preferred_element_type=jnp.float32,
        )
        centre = jnp.sum(probabilities * prob_grad, axis=-1, keepdims=True)
        score_grad = (probabilities * (prob_grad - centre)).astype(jnp.bfloat16)
        query_part = (
            jnp.einsum("hqk,khd->qhd", score_grad, key_heads, preferred_element_type=jnp.float32)
            * score_scale
        )
        key_acc = (
            key_acc
            + jnp.einsum(
                "hqk,qhd->khd", score_grad, query_block, preferred_element_type=jnp.float32
            )
            * score_scale
        )
        return ((key_acc, value_acc), query_part)

    zeros_init = jnp.zeros((length, per_dev, head_width), jnp.float32)
    (key_acc, value_acc), query_parts = lax.scan(
        backward_block, (zeros_init, zeros_init), jnp.arange(block_count, dtype=jnp.int32)
    )
    query_rot_grad = query_parts.reshape(length, per_dev, head_width)
    unused_query, query_back = jax.vjp(
        lambda raw_proj, gain_vec: head_prep(raw_proj, gain_vec, cosine, sine_table),
        query_raw,
        gain_query,
    )
    query_raw_grad, gain_query_grad = query_back(query_rot_grad)
    query_low = query_raw_grad.astype(jnp.bfloat16)
    key_group_grad = jnp.einsum("lhd,hg->lgd", key_acc, group_pick, precision=lax.Precision.HIGHEST)
    value_group_grad = jnp.einsum(
        "lhd,hg->lgd", value_acc, group_pick, precision=lax.Precision.HIGHEST
    )
    unused_key, key_back = jax.vjp(
        lambda raw_proj, gain_vec: head_prep(raw_proj, gain_vec, cosine, sine_table),
        key_f32,
        gain_key,
    )
    key_raw_grad, gain_key_grad = key_back(key_group_grad)
    key_low = key_raw_grad.astype(jnp.bfloat16)
    value_low = value_group_grad.reshape(length, groups_dev * head_width).astype(jnp.bfloat16)
    grad_query = matmul_tn(attn_in, query_low)
    grad_key = matmul_tn(attn_in, key_low)
    grad_value = matmul_tn(attn_in, value_low)
    attn_in_grad = lax.psum_scatter(
        (
            matmul_nt(query_low, w_query)
            + matmul_nt(key_low, w_key)
            + matmul_nt(value_low, w_value)
        ).astype(jnp.bfloat16),
        "tensor",
        scatter_dimension=0,
        tiled=True,
    ).astype(jnp.float32)
    unused_attn, attn_norm_back = jax.vjp(norm_gain, input_f32, gain_attn)
    input_part, gain_attn_grad = attn_norm_back(attn_in_grad)
    input_grad = (input_part + residual_grad).astype(jnp.bfloat16)
    reduced = (
        lax.psum_scatter(
            grad_query.astype(jnp.bfloat16), "dp", scatter_dimension=0, tiled=True
        ).astype(jnp.float32),
        lax.psum_scatter(
            grad_key.astype(jnp.bfloat16), "dp", scatter_dimension=0, tiled=True
        ).astype(jnp.float32),
        lax.psum_scatter(
            grad_value.astype(jnp.bfloat16), "dp", scatter_dimension=0, tiled=True
        ).astype(jnp.float32),
        lax.psum_scatter(
            grad_out.astype(jnp.bfloat16), "dp", scatter_dimension=1, tiled=True
        ).astype(jnp.float32),
        lax.psum_scatter(
            grad_gate.astype(jnp.bfloat16), "dp", scatter_dimension=0, tiled=True
        ).astype(jnp.float32),
        lax.psum_scatter(
            grad_up.astype(jnp.bfloat16), "dp", scatter_dimension=0, tiled=True
        ).astype(jnp.float32),
        lax.psum_scatter(
            grad_down.astype(jnp.bfloat16), "dp", scatter_dimension=1, tiled=True
        ).astype(jnp.float32),
    )
    gain_sums = lax.psum(
        (gain_attn_grad, gain_ffn_grad, gain_query_grad, gain_key_grad), ("dp", "tensor")
    )
    return (
        layer_out,
        input_grad,
        reduced[0],
        reduced[1],
        reduced[2],
        reduced[3],
        reduced[4],
        reduced[5],
        reduced[6],
        gain_sums[0],
        gain_sums[1],
        gain_sums[2],
        gain_sums[3],
    )


def solution(mesh):
    in_specs = (
        P(("dp", "tensor"), None),
        P("dp", None),
        P(None, "tensor"),
        P(None, "tensor"),
        P(None, "tensor"),
        P("tensor", None),
        P(None, "tensor"),
        P(None, "tensor"),
        P("tensor", None),
        P(),
        P(),
        P(),
        P(),
        P(("dp", "tensor"), None),
    )
    out_specs = (
        P(("dp", "tensor"), None),
        P(("dp", "tensor"), None),
        P("dp", "tensor"),
        P("dp", "tensor"),
        P("dp", "tensor"),
        P("tensor", "dp"),
        P("dp", "tensor"),
        P("dp", "tensor"),
        P("tensor", "dp"),
        P(),
        P(),
        P(),
        P(),
    )
    return jax.shard_map(
        per_device, mesh=mesh, in_specs=in_specs, out_specs=out_specs, check_vma=False
    )
```

profile of v0, /device:TPU:18, one launch (start us, length us, event | category | flops | bytes accessed | tf_op | source)
XLA Modules:
  0.0 1040.6 jit_solution(6680544151590472490)
XLA Ops:
  7.3 1.4 fusion.31
  8.7 2.0 fusion.23
  10.8 0.8 reduce-window.8
  12.7 0.9 fusion.36
  13.6 20.0 %all-gather.5.cloned.1.call-done = bf16[512,2048]{1,0:T(8,128)(2,1)} async-done(((bf16[128,2048]{1,0:T(8,128)(2,1)}), bf16[512,2048]{1,0:T(8,128)(2,1)}) %all-gather.5.cloned.1.call-update) | async-done | bytes 2097168 | tf_op jit(solution)/shard_map/all_gather | solution.py:91
  33.6 2.7 fusion.46
  37.4 0.8 convolution_convert_fusion.13
  38.6 1.3 multiply_reduce_fusion.4
  40.5 1.8 fusion.64
  42.3 1.2 fusion
  43.5 2.0 copy-done.1
  45.6 1.6 fusion.15
  47.2 2.6 convolution_convert_fusion.6
  49.8 31.5 %reduce-scatter.12.cloned.1.call-done = bf16[128,2048]{1,0:T(8,128)(2,1)} async-done(((bf16[512,2048]{1,0:T(8,128)(2,1)}), bf16[128,2048]{1,0:T(8,128)(2,1)}) %reduce-scatter.12.cloned.1.call-update) | async-done | bytes 524304 | tf_op jit(solution)/shard_map/reduce_scatter | solution.py:145
  81.4 1.3 multiply_reduce_fusion.3
  82.7 2.0 multiply_convert_fusion.3
  85.9 21.6 %all-gather.7.cloned.1.call-done = bf16[512,2048]{1,0:T(8,128)(2,1)} async-done(((bf16[128,2048]{1,0:T(8,128)(2,1)}), bf16[512,2048]{1,0:T(8,128)(2,1)}) %all-gather.7.cloned.1.call-update) | async-done | bytes 2097168 | tf_op jit(solution)/shard_map/all_gather | solution.py:151
  107.5 10.6 %fusion.66 = f32[512,2048]{1,0:T(8,128)} fusion(bf16[512,2048]{1,0:T(8,128)(2,1)} %all-gather.7.cloned.1.call-done, bf16[2048,2048]{1,0:T(8,128)(2,1)} %param.21), kind=kOutput, calls=%fused_computation.150 | convolution fusion | flops 4294967296 | bytes 14680064 | tf_op jit(solution)/shard_map/dot_general | solution.py:155
  118.1 9.5 fusion.65
  127.6 4.1 all-gather.9.cloned.1.call-done
  131.6 13.6 %multiply_convert_fusion.1 = (bf16[512,2048]{1,0:T(8,128)(2,1)S(1)}, bf16[512,2048]{1,0:T(8,128)(2,1)S(1)}, bf16[512,2048]{1,0:T(8,128)(2,1)}) fusion(f32[512,2048]{1,0:T(8,128)} %fusion.65, f32[512,2048]{1,0:T(8,128)} %fusion.66, bf16[512,2048]{1,0:T(8,128)(2,1)} %all-gather.9.cloned.1.call-done, bf16[2048,2048]{1,0:T(8,128)(2,1)} %param.22), kind=kOutput, calls=%fused_computation.18 | convolution fusion | flops 4311744512 | bytes 25165824 | tf_op jit(solution)/shard_map/dot_general | solution.py:55
  145.2 8.5 fusion.67
  153.7 9.2 add_convert_fusion.1
  163.2 31.4 %reduce-scatter.16.cloned.1.call-done = bf16[128,2048]{1,0:T(8,128)(2,1)} async-done(((bf16[512,2048]{1,0:T(8,128)(2,1)}), bf16[128,2048]{1,0:T(8,128)(2,1)}) %reduce-scatter.16.cloned.1.call-update) | async-done | bytes 524304 | tf_op jit(solution)/shard_map/reduce_scatter | solution.py:175
  194.6 2.1 fusion.25
  196.7 2.4 fusion.63
  199.3 22.7 %all-gather.11.cloned.1.call-done = bf16[512,2048]{1,0:T(8,128)(2,1)} async-done(((bf16[128,2048]{1,0:T(8,128)(2,1)}), bf16[512,2048]{1,0:T(8,128)(2,1)}) %all-gather.11.cloned.1.call-update) | async-done | bytes 2097168 | tf_op jit(solution)/shard_map/all_gather | solution.py:184
  221.9 3.6 convolution_convert_fusion.9
  225.6 5.0 fusion.10
  230.6 4.9 multiply_reduce_fusion
  235.5 1.2 fusion.22
  236.7 1.6 convolution_convert_fusion.7
  238.4 6.7 multiply_convert_fusion
  245.2 1.4 fusion.13
  246.6 1.2 fusion.34
  249.4 1.6 convolution_convert_fusion.8
  251.0 4.3 convolution_convert_fusion.3
  255.7 3.3 fusion.14
  259.9 0.8 copy-done.11
  260.7 2.7 convolution_convert_fusion.4
  263.5 1.8 fusion.69
  265.3 1.3 fusion.68
  266.6 2.1 add_convert_fusion
  268.8 9.8 convolution_convert_fusion.5
  279.1 10.1 convolution_convert_fusion
  289.2 10.0 convolution_convert_fusion.1
  299.5 10.1 convolution_convert_fusion.2
  309.7 1.5 convert_element_type.229
  311.2 54.5 %reduce-scatter.22.cloned.1.call-done = bf16[256,128]{1,0:T(8,128)(2,1)} async-done(((bf16[2048,128]{1,0:T(8,128)(2,1)}), bf16[256,128]{1,0:T(8,128)(2,1)}) %reduce-scatter.22.cloned.1.call-update) | async-done | bytes 65552 | tf_op jit(solution)/shard_map/reduce_scatter | solution.py:261
  365.7 1.5 convert_element_type.227
  367.2 69.3 %reduce-scatter.26.cloned.1.call-done = bf16[512,256]{1,0:T(8,128)(2,1)} async-done(((bf16[512,2048]{1,0:T(8,128)(2,1)}), bf16[512,256]{1,0:T(8,128)(2,1)}) %reduce-scatter.26.cloned.1.call-update) | async-done | bytes 262160 | tf_op jit(solution)/shard_map/reduce_scatter | solution.py:267
  436.5 1.8 convert_element_type.231
  438.2 68.2 %reduce-scatter.20.cloned.1.call-done = bf16[256,512]{1,0:T(8,128)(2,1)} async-done(((bf16[2048,512]{1,0:T(8,128)(2,1)}), bf16[256,512]{1,0:T(8,128)(2,1)}) %reduce-scatter.20.cloned.1.call-update) | async-done | bytes 262160 | tf_op jit(solution)/shard_map/reduce_scatter | solution.py:258
  506.4 1.8 convert_element_type.225
  508.2 31.9 %reduce-scatter.18.cloned.1.call-done = bf16[128,2048]{1,0:T(8,128)(2,1)} async-done(((bf16[512,2048]{1,0:T(8,128)(2,1)}), bf16[128,2048]{1,0:T(8,128)(2,1)}) %reduce-scatter.18.cloned.1.call-update) | async-done | bytes 524304 | tf_op jit(solution)/shard_map/reduce_scatter | solution.py:244
  540.1 1.6 fusion.26
  541.7 41.4 %all-reduce.4 = (f32[2048]{0:T(1024)}, f32[2048]{0:T(1024)}, f32[64]{0:T(128)}, f32[64]{0:T(128)}) all-reduce(f32[2048]{0:T(1024)S(1)} %get-tuple-element.63, f32[2048]{0:T(1024)S(1)} %copy-done.35, f32[64]{0:T(128)S(1)} %get-tuple-element.61, f32[64]{0:T(128)S(1)} %copy-done.46), channel_id=1, replica_groups=mesh['dp'=8,'tensor'=4] {'dp','tensor'}, use_global_device_ids=true, to_apply=%region_26.27 | all-reduce | flops 4224 | bytes 33792 | tf_op jit(solution)/shard_map/psum | solution.py:280
  583.1 3.4 fusion.30
  586.5 141.1 %reduce-scatter.32.cloned.1.call-done = bf16[2048,256]{1,0:T(8,128)(2,1)} async-done(((bf16[2048,2048]{1,0:T(8,128)(2,1)}), bf16[2048,256]{1,0:T(8,128)(2,1)}) %reduce-scatter.32.cloned.1.call-update) | async-done | bytes 1048592 | tf_op jit(solution)/shard_map/reduce_scatter | solution.py:276
  727.6 2.7 convert_element_type.237
  730.3 149.3 %reduce-scatter.30.cloned.1.call-done = bf16[256,2048]{1,0:T(8,128)(2,1)} async-done(((bf16[2048,2048]{1,0:T(8,128)(2,1)}), bf16[256,2048]{1,0:T(8,128)(2,1)}) %reduce-scatter.30.cloned.1.call-update) | async-done | bytes 1048592 | tf_op jit(solution)/shard_map/reduce_scatter | solution.py:273
  879.6 2.8 convert_element_type.235
  882.3 148.8 %reduce-scatter.28.cloned.1.call-done = bf16[256,2048]{1,0:T(8,128)(2,1)} async-done(((bf16[2048,2048]{1,0:T(8,128)(2,1)}), bf16[256,2048]{1,0:T(8,128)(2,1)}) %reduce-scatter.28.cloned.1.call-update) | async-done | bytes 1048592 | tf_op jit(solution)/shard_map/reduce_scatter | solution.py:270
  1031.1 2.8 convert_element_type.233
  (176 shorter events, 8.5 us)
Async XLA Ops:
  7.2 31.4 %copy-start = (bf16[2048,512]{1,0:T(8,128)(2,1)S(1)}, bf16[2048,512]{1,0:T(8,128)(2,1)}, u32[]{:S(2)}) copy-start(bf16[2048,512]{1,0:T(8,128)(2,1)} %param.16) | copy-start | bytes 6291460
  7.2 29.1 %copy-start.42 = (f32[64]{0:T(128)S(1)}, f32[64]{0:T(128)}, u32[]{:S(2)}) copy-start(f32[64]{0:T(128)} %param.26) | copy-start | bytes 772
  7.2 30.1 %copy-start.15 = (bf16[2048,128]{1,0:T(8,128)(2,1)S(1)}, bf16[2048,128]{1,0:T(8,128)(2,1)}, u32[]{:S(2)}) copy-start(bf16[2048,128]{1,0:T(8,128)(2,1)} %param.18) | copy-start | bytes 1572868
  7.2 26.4 %all-gather.5.cloned.1.call-start = ((), (), s32[]{:S(2)}) async-start(), calls=%async_computation.11 | async-start | bytes 2621440 | tf_op jit(solution)/shard_map/all_gather | solution.py:91
  8.6 3.7 copy-start.49
  8.7 3.0 copy-start.44
  10.7 70.7 %reduce-scatter.12.cloned.1.call-start = ((), (), s32[]{:S(2)}) async-start(), calls=%async_computation.12 | async-start | bytes 2621440 | tf_op jit(solution)/shard_map/reduce_scatter | solution.py:145
  11.6 223.9 %copy-start.36 = (s32[8]{0:T(128)}, s32[8]{0:T(128)S(1)}, u32[]{:S(2)}) copy-start(s32[8]{0:T(128)S(1)} %and_select_fusion) | copy-start | bytes 100
  33.6 3.7 copy-start.2
  37.4 3.1 copy-start.17
  38.6 4.9 copy-start.13
  38.6 1.9 copy-start.24
  39.9 2.3 copy-start.8
  40.0 2.3 copy-start.31
  40.4 1.8 copy-start.20
  40.5 1.8 copy-start.22
  42.3 3.3 copy-start.1
  47.1 35.5 %copy-start.53 = (bf16[8,64,512]{2,1,0:T(8,128)(2,1)}, bf16[8,64,512]{2,1,0:T(8,128)(2,1)S(1)}, u32[]{:S(2)}) copy-start(bf16[8,64,512]{2,1,0:T(8,128)(2,1)S(1)} %fusion.15) | copy-start | bytes 1572868
  47.1 34.2 %copy-start.7 = (bf16[128,2048]{1,0:T(8,128)(2,1)S(1)}, bf16[128,2048]{1,0:T(8,128)(2,1)}, u32[]{:S(2)}) copy-start(bf16[128,2048]{1,0:T(8,128)(2,1)} %param.14) | copy-start | bytes 1572868
  47.2 35.5 %copy-start.26 = (f32[2048]{0:T(1024)S(1)}, f32[2048]{0:T(1024)}, u32[]{:S(2)}) copy-start(f32[2048]{0:T(1024)} %param.24) | copy-start | bytes 24580
  49.8 57.7 %all-gather.7.cloned.1.call-start = ((), (), s32[]{:S(2)}) async-start(), calls=%async_computation.13 | async-start | bytes 2621440 | tf_op jit(solution)/shard_map/all_gather | solution.py:151
  82.7 114.0 %copy-start.38 = (f32[128]{0:T(128)}, f32[128]{0:T(128)S(1)}, u32[]{:S(2)}) copy-start(f32[128]{0:T(128)S(1)} %fusion.58) | copy-start | bytes 1540
  84.8 46.9 %all-gather.9.cloned.1.call-start = ((), (), s32[]{:S(2)}) async-start(), calls=%async_computation.15 | async-start | bytes 2621440 | tf_op jit(solution)/shard_map/all_gather | solution.py:166
  85.4 109.2 %reduce-scatter.16.cloned.1.call-start = ((), (), s32[]{:S(2)}) async-start(), calls=%async_computation.16 | async-start | bytes 2621440 | tf_op jit(solution)/shard_map/reduce_scatter | solution.py:175
  107.5 10.6 %copy-start.52 = (bf16[512,2048]{1,0:T(8,128)(2,1)S(1)}, bf16[512,2048]{1,0:T(8,128)(2,1)}, u32[]{:S(2)}) copy-start(bf16[512,2048]{1,0:T(8,128)(2,1)} %all-gather.7.cloned.1.call-done) | copy-start | bytes 6291460
  145.2 8.5 copy-start.54
  145.2 8.5 copy-start.55
  153.7 40.9 %copy-start.10 = (bf16[128,2048]{1,0:T(8,128)(2,1)S(1)}, bf16[128,2048]{1,0:T(8,128)(2,1)}, u32[]{:S(2)}) copy-start(bf16[128,2048]{1,0:T(8,128)(2,1)} %reduce-scatter.12.cloned.1.call-done) | copy-start | bytes 1572868
  163.0 58.9 %all-gather.11.cloned.1.call-start = ((), (), s32[]{:S(2)}) async-start(), calls=%async_computation.17 | async-start | bytes 2621440 | tf_op jit(solution)/shard_map/all_gather | solution.py:184
  196.7 2.5 copy-start.47
  199.2 110.5 %reduce-scatter.24.cloned.1.call-start = ((), (), s32[]{:S(2)}) async-start(), calls=%async_computation.21 | async-start | bytes 589824 | tf_op jit(solution)/shard_map/reduce_scatter | solution.py:264
  199.3 31.3 %copy-start.25 = (f32[8,512]{1,0:T(8,128)}, f32[8,512]{1,0:T(8,128)S(1)}, u32[]{:S(2)}) copy-start(f32[8,512]{1,0:T(8,128)S(1)} %log_add_fusion) | copy-start | bytes 49156
  221.9 8.7 slice-start
  225.6 5.0 slice-start.1
  225.6 5.0 copy-start.14
  230.6 6.1 copy-start.3
  238.3 127.4 %reduce-scatter.22.cloned.1.call-start = ((), (), s32[]{:S(2)}) async-start(), calls=%async_computation.20 | async-start | bytes 589824 | tf_op jit(solution)/shard_map/reduce_scatter | solution.py:261
  238.4 6.8 copy-start.21
  238.4 6.8 copy-start.23
  245.1 3.4 copy-start.6
  245.2 2.7 copy-start.30
  245.2 2.7 copy-start.43
  245.2 3.4 copy-start.34
  245.2 4.2 copy-start.4
  250.9 185.5 %reduce-scatter.26.cloned.1.call-start = ((), (), s32[]{:S(2)}) async-start(), calls=%async_computation.22 | async-start | bytes 2359296 | tf_op jit(solution)/shard_map/reduce_scatter | solution.py:267
  255.4 3.8 copy-start.41
  255.4 4.2 copy-start.32
  255.4 251.0 %reduce-scatter.20.cloned.1.call-start = ((), (), s32[]{:S(2)}) async-start(), calls=%async_computation.19 | async-start | bytes 2359296 | tf_op jit(solution)/shard_map/reduce_scatter | solution.py:258
  255.6 3.5 copy-start.9
  260.7 2.7 copy-start.19
  263.4 276.7 %reduce-scatter.18.cloned.1.call-start = ((), (), s32[]{:S(2)}) async-start(), calls=%async_computation.18 | async-start | bytes 2621440 | tf_op jit(solution)/shard_map/reduce_scatter | solution.py:244
  263.4 1.8 copy-start.12
  268.7 314.4 %reduce-scatter.14.cloned.1.call-start = ((), (), s32[]{:S(2)}) async-start(), calls=%async_computation.14 | async-start | bytes 2621440 | tf_op jit(solution)/shard_map/reduce_scatter | solution.py:159
  278.6 449.0 %reduce-scatter.32.cloned.1.call-start = ((), (), s32[]{:S(2)}) async-start(), calls=%async_computation.25 | async-start | bytes 9437184 | tf_op jit(solution)/shard_map/reduce_scatter | solution.py:276
  289.2 590.4 %reduce-scatter.30.cloned.1.call-start = ((), (), s32[]{:S(2)}) async-start(), calls=%async_computation.24 | async-start | bytes 9437184 | tf_op jit(solution)/shard_map/reduce_scatter | solution.py:273
  299.3 731.8 %reduce-scatter.28.cloned.1.call-start = ((), (), s32[]{:S(2)}) async-start(), calls=%async_computation.23 | async-start | bytes 9437184 | tf_op jit(solution)/shard_map/reduce_scatter | solution.py:270
  309.6 230.5 %copy-start.28 = (f32[2048]{0:T(1024)S(1)}, f32[2048]{0:T(1024)}, u32[]{:S(2)}) copy-start(f32[2048]{0:T(1024)} %param.23) | copy-start | bytes 24580
  309.6 230.5 %copy-start.45 = (f32[128]{0:T(128)S(1)}, f32[128]{0:T(128)}, u32[]{:S(2)}) copy-start(f32[128]{0:T(128)} %copy-done.44) | copy-start | bytes 1540
  309.6 232.1 %copy-start.35 = (f32[2048]{0:T(1024)S(1)}, f32[2048]{0:T(1024)}, u32[]{:S(2)}) copy-start(f32[2048]{0:T(1024)} %get-tuple-element.59) | copy-start | bytes 24580
  309.6 232.1 %copy-start.46 = (f32[64]{0:T(128)S(1)}, f32[64]{0:T(128)}, u32[]{:S(2)}) copy-start(f32[64]{0:T(128)} %get-tuple-element.76) | copy-start | bytes 772
  309.6 273.5 %copy-start.50 = (f32[128]{0:T(128)S(1)}, f32[128]{0:T(128)}, u32[]{:S(2)}) copy-start(f32[128]{0:T(128)} %copy-done.49) | copy-start | bytes 1540
  309.6 273.5 %copy-start.27 = (f32[2048]{0:T(1024)S(1)}, f32[2048]{0:T(1024)}, u32[]{:S(2)}) copy-start(f32[2048]{0:T(1024)} %param.24) | copy-start | bytes 24580
  309.6 273.5 %copy-start.39 = (f32[128]{0:T(128)S(1)}, f32[128]{0:T(128)}, u32[]{:S(2)}) copy-start(f32[128]{0:T(128)} %copy-done.38) | copy-start | bytes 1540
  309.6 273.5 %copy-start.48 = (f32[128]{0:T(128)S(1)}, f32[128]{0:T(128)}, u32[]{:S(2)}) copy-start(f32[128]{0:T(128)} %copy-done.47) | copy-start | bytes 1540
  (9 other events, 10.2 us)
Sparse Core Ops, SparseCore 0:
  10.8 22.7 all-gather.4
  49.9 31.4 reduce-scatter.11
  84.9 22.5 all-gather.6
  109.0 22.5 all-gather.8
  163.1 31.4 reduce-scatter.15
  199.3 22.5 all-gather.10
  238.4 61.8 reduce-scatter.23
  304.6 61.0 reduce-scatter.21
  369.2 67.1 reduce-scatter.25
  439.9 66.5 reduce-scatter.19
  509.5 30.5 reduce-scatter.17
  543.2 31.5 reduce-scatter.13
  578.4 149.1 reduce-scatter.31
  731.5 147.9 reduce-scatter.29
  883.0 148.0 reduce-scatter.27
where the time goes:
time: 1050 us; the launch traced here: 1040 us
  waiting for transfers between devices  795 us (76%)
  matrix products  139 us (13%)
  other arithmetic  44.3 us (4%)
  blocking collectives  41.4 us (4%)
  between operations  15.1 us (1%)
    reduce_scatter x1, waiting for transfers between devices, per_device(): lax.psum_scatter(grad_up.astype(jnp.bfloat16), 'dp', scatter_dimension=0,...  149 us
    reduce_scatter x1, waiting for transfers between devices, per_device(): lax.psum_scatter(grad_gate.astype(jnp.bfloat16), 'dp', scatter_dimension=...  149 us
    reduce_scatter x1, waiting for transfers between devices, per_device(): lax.psum_scatter(grad_down.astype(jnp.bfloat16), 'dp', scatter_dimension=...  141 us
    reduce_scatter x1, waiting for transfers between devices, per_device(): lax.psum_scatter(grad_out.astype(jnp.bfloat16), 'dp', scatter_dimension=1...  69.3 us
    reduce_scatter x1, waiting for transfers between devices, per_device(): lax.psum_scatter(grad_query.astype(jnp.bfloat16), 'dp', scatter_dimension...  68.2 us
    reduce_scatter x1, waiting for transfers between devices, per_device(): lax.psum_scatter(grad_key.astype(jnp.bfloat16), 'dp', scatter_dimension=0...  54.5 us
    psum x1, blocking collectives, per_device(): lax.psum((gain_attn_grad, gain_ffn_grad, gain_query_grad, gain_key_grad),...  41.4 us
    dot_general x7, matrix products, matmul_tn(): lax.dot_general(left_mat, right_mat, (((0,), (0,)), ((), ())), preferred_...  40.3 us
  transfers between devices with their start and end apart: 15, of which 13 were waited for; matrix products, arithmetic and copies ran while one was open for 10% of the time, Pallas kernels for 0%

commit v1 on v0

--- a/solution.py
+++ b/solution.py
@@ -1,6 +1,8 @@
 import jax
 import jax.numpy as jnp
 from jax import lax
+from jax.experimental import pallas as pl
+from jax.experimental.pallas import tpu as pltpu
 from jax.sharding import PartitionSpec as P
 
 HEADS = 32
@@ -297,6 +299,1032 @@
     )
 
 
+def dp_shape():
+    total = lax.axis_size("dp")
+    z_count = 4 if total % 4 == 0 else total
+    return (z_count, total // z_count)
+
+
+def dp_place():
+    z_count, y_count = dp_shape()
+    me = lax.axis_index("dp")
+    return (me // y_count, me % y_count)
+
+
+def own_slices(array, dim, index):
+    z_count, y_count = dp_shape()
+    shape = array.shape
+    width = shape[dim] // (z_count * y_count)
+    split = array.reshape(shape[:dim] + (z_count, y_count, width) + shape[dim + 1 :])
+    part = lax.dynamic_index_in_dim(split, index, dim + 1, keepdims=False)
+    return part.reshape(shape[:dim] + (z_count * width,) + shape[dim + 1 :])
+
+
+def y_shift(array, distance):
+    z_count, y_count = dp_shape()
+    pairs = [
+        (z * y_count + y, z * y_count + (y + distance) % y_count)
+        for z in range(z_count)
+        for y in range(y_count)
+    ]
+    return lax.ppermute(array, "dp", pairs)
+
+
+def pair_product(left, right, dim):
+    z_count, y_count = dp_shape()
+    y_me = dp_place()[1]
+    shared, full = (left, right) if dim == 0 else (right, left)
+    total = None
+    for distance in range(y_count):
+        target = (y_me + distance) % y_count
+        own = own_slices(shared, 1, target)
+        rest = full
+        if distance:
+            own, rest = y_shift(own, distance), y_shift(full, distance)
+        term = matmul_tn(own, rest) if dim == 0 else matmul_tn(rest, own)
+        total = term if total is None else total + term
+    return total.astype(jnp.bfloat16)
+
+
+def pair_sum(left, right, dim):
+    z_count, y_count = dp_shape()
+    y_me = dp_place()[1]
+    product = matmul_tn(left, right)
+    total = own_slices(product, dim, y_me)
+    for distance in range(1, y_count):
+        part = own_slices(product, dim, (y_me + distance) % y_count).astype(jnp.bfloat16)
+        total = total + y_shift(part, distance).astype(jnp.float32)
+    return total.astype(jnp.bfloat16)
+
+
+def line_reduce(partial, dim):
+    z_count, y_count = dp_shape()
+    z_me = dp_place()[0]
+    shape = partial.shape
+    blocks = partial.reshape(
+        shape[:dim] + (z_count, shape[dim] // z_count) + shape[dim + 1 :]
+    )
+
+    def block(index):
+        return lax.dynamic_index_in_dim(
+            blocks, jnp.clip(index, 0, z_count - 1), dim, keepdims=False
+        )
+
+    def chain(step_of, place, block_of):
+        arrived = None
+        for step in range(z_count - 1):
+            send = block(block_of(z_count - 1 - step + place(z_me)))
+            if arrived is not None:
+                send = (send.astype(jnp.float32) + arrived.astype(jnp.float32)).astype(
+                    jnp.bfloat16
+                )
+            pairs = [
+                (z * y_count + y, (z + step_of) * y_count + y)
+                for z in range(z_count)
+                for y in range(y_count)
+                if place(z) <= step
+            ]
+            arrived = lax.ppermute(send, "dp", pairs)
+        return arrived
+
+    from_low = chain(1, lambda z: z, lambda index: index)
+    from_high = chain(-1, lambda z: z_count - 1 - z, lambda index: z_count - 1 - index)
+    return (
+        block(z_me).astype(jnp.float32)
+        + from_low.astype(jnp.float32)
+        + from_high.astype(jnp.float32)
+    )
+
+
+def attention_forward(attn_in, doc_lengths, w_query, w_key, w_value, gain_query, gain_key):
+    head_width = gain_query.shape[0]
+    length = attn_in.shape[0]
+    per_dev = w_query.shape[1] // head_width
+    groups_dev = w_key.shape[1] // head_width
+    doc_ids, places, offsets = doc_layout(doc_lengths[0], length)
+    cosine, sine_table = rope_tables(offsets, head_width)
+    query_raw = jnp.dot(attn_in, w_query, preferred_element_type=jnp.float32)
+    key_raw = jnp.dot(attn_in, w_key, preferred_element_type=jnp.float32).astype(jnp.bfloat16)
+    value_raw = jnp.dot(attn_in, w_value, preferred_element_type=jnp.float32).astype(jnp.bfloat16)
+    key_f32 = key_raw.astype(jnp.float32)
+    queries = head_prep(query_raw, gain_query, cosine, sine_table).astype(jnp.bfloat16)
+    key_rot = head_prep(key_f32, gain_key, cosine, sine_table).astype(jnp.bfloat16)
+    local_heads = jnp.arange(per_dev, dtype=jnp.int32)
+    group_pick = (
+        local_heads[:, None] // (HEADS // KV) == jnp.arange(groups_dev, dtype=jnp.int32)[None, :]
+    ).astype(jnp.float32)
+    pick_low = group_pick.astype(jnp.bfloat16)
+    key_heads = jnp.einsum(
+        "lgd,hg->lhd", key_rot, pick_low, preferred_element_type=jnp.float32
+    ).astype(jnp.bfloat16)
+    value_heads = jnp.einsum(
+        "lgd,hg->lhd",
+        value_raw.reshape(length, groups_dev, head_width),
+        pick_low,
+        preferred_element_type=jnp.float32,
+    ).astype(jnp.bfloat16)
+    block_rows = min(512, length)
+    block_count = length // block_rows
+    score_scale = head_width ** (-0.5)
+
+    def block_scores(block_num):
+        row_begin = block_num * block_rows
+        query_block = lax.dynamic_slice_in_dim(queries, row_begin, block_rows, 0)
+        ids_block = lax.dynamic_slice_in_dim(doc_ids, row_begin, block_rows, 0)
+        places_block = lax.dynamic_slice_in_dim(places, row_begin, block_rows, 0)
+        scores = (
+            jnp.einsum("qhd,khd->hqk", query_block, key_heads, preferred_element_type=jnp.float32)
+            * score_scale
+        )
+        allowed = (ids_block[:, None] == doc_ids[None, :]) & (
+            places[None, :] <= places_block[:, None]
+        )
+        return (query_block, jnp.where(allowed[None], scores, MASKED))
+
+    def forward_block(block_num):
+        query_block, scores = block_scores(block_num)
+        row_top = jnp.max(scores, axis=-1, keepdims=True)
+        exponent = jnp.exp(scores - row_top)
+        row_total = jnp.sum(exponent, axis=-1, keepdims=True)
+        probabilities = (exponent / row_total).astype(jnp.bfloat16)
+        mixed_block = jnp.einsum(
+            "hqk,khd->qhd", probabilities, value_heads, preferred_element_type=jnp.float32
+        )
+        return (mixed_block, row_top + jnp.log(row_total))
+
+    mixed_all, log_totals = lax.map(forward_block, jnp.arange(block_count, dtype=jnp.int32))
+    attn_mixed = mixed_all.reshape(length, per_dev * head_width).astype(jnp.bfloat16)
+    saved = (
+        block_scores,
+        log_totals,
+        (key_heads, value_heads, queries),
+        (query_raw, key_f32, cosine, sine_table, group_pick),
+    )
+    return (attn_mixed, saved)
+
+
+def attention_backward(mixed_grad, saved, gain_query, gain_key):
+    block_scores, log_totals, heads, rest = saved
+    key_heads, value_heads, queries = heads
+    query_raw, key_f32, cosine, sine_table, group_pick = rest
+    length, per_dev, head_width = queries.shape
+    groups_dev = group_pick.shape[1]
+    block_rows = min(512, length)
+    block_count = length // block_rows
+    score_scale = head_width ** (-0.5)
+    mixed_grad = mixed_grad.reshape(length, per_dev, head_width)
+
+    def backward_block(running, block_num):
+        key_acc, value_acc = running
+        query_block, scores = block_scores(block_num)
+        probabilities = jnp.exp(scores - log_totals[block_num])
+        grad_block = lax.dynamic_slice_in_dim(mixed_grad, block_num * block_rows, block_rows, 0)
+        prob_grad = jnp.einsum(
+            "qhd,khd->hqk", grad_block, value_heads, preferred_element_type=jnp.float32
+        )
+        value_acc = value_acc + jnp.einsum(
+            "hqk,qhd->khd",
+            probabilities.astype(jnp.bfloat16),
+            grad_block,
+            preferred_element_type=jnp.float32,
+        )
+        centre = jnp.sum(probabilities * prob_grad, axis=-1, keepdims=True)
+        score_grad = (probabilities * (prob_grad - centre)).astype(jnp.bfloat16)
+        query_part = (
+            jnp.einsum("hqk,khd->qhd", score_grad, key_heads, preferred_element_type=jnp.float32)
+            * score_scale
+        )
+        key_acc = (
+            key_acc
+            + jnp.einsum(
+                "hqk,qhd->khd", score_grad, query_block, preferred_element_type=jnp.float32
+            )
+            * score_scale
+        )
+        return ((key_acc, value_acc), query_part)
+
+    zeros_init = jnp.zeros((length, per_dev, head_width), jnp.float32)
+    (key_acc, value_acc), query_parts = lax.scan(
+        backward_block, (zeros_init, zeros_init), jnp.arange(block_count, dtype=jnp.int32)
+    )
+    query_rot_grad = query_parts.reshape(length, per_dev, head_width)
+    unused_query, query_back = jax.vjp(
+        lambda raw_proj, gain_vec: head_prep(raw_proj, gain_vec, cosine, sine_table),
+        query_raw,
+        gain_query,
+    )
+    query_raw_grad, gain_query_grad = query_back(query_rot_grad)
+    query_low = query_raw_grad.astype(jnp.bfloat16)
+    key_group_grad = jnp.einsum("lhd,hg->lgd", key_acc, group_pick, precision=lax.Precision.HIGHEST)
+    value_group_grad = jnp.einsum(
+        "lhd,hg->lgd", value_acc, group_pick, precision=lax.Precision.HIGHEST
+    )
+    unused_key, key_back = jax.vjp(
+        lambda raw_proj, gain_vec: head_prep(raw_proj, gain_vec, cosine, sine_table),
+        key_f32,
+        gain_key,
+    )
+    key_raw_grad, gain_key_grad = key_back(key_group_grad)
+    key_low = key_raw_grad.astype(jnp.bfloat16)
+    value_low = value_group_grad.reshape(length, groups_dev * head_width).astype(jnp.bfloat16)
+    return (query_low, key_low, value_low, gain_query_grad, gain_key_grad)
+
+
+MESH_ID = pl.DeviceIdType.MESH
+ORDERS = (("x", "y", "z"), ("y", "z", "x"), ("z", "x", "y"))
+LINKS = ("x", "y", "z", "core")
+F32 = jnp.float32
+BF16 = jnp.bfloat16
+
+
+class Place:
+    def __init__(self):
+        row, column = lax.axis_index("dp"), lax.axis_index("tensor")
+        self.far = row // 4
+        self.at = {
+            "z": (row // 2) % 2,
+            "y": row % 2,
+            "x": column // 2,
+            "core": column % 2,
+        }
+
+    def flipped(self, names):
+        return {
+            name: 1 - value if name in names else value for name, value in self.at.items()
+        }
+
+    def device(self, name):
+        at = self.flipped((name,))
+        return {
+            "dp": self.far * 4 + at["z"] * 2 + at["y"],
+            "tensor": at["x"] * 2 + at["core"],
+        }
+
+    def column(self, names=()):
+        at = self.flipped(names)
+        return at["x"] * 2 + at["core"]
+
+    def quarter(self):
+        return self.at["z"] * 2 + self.at["y"]
+
+
+def enter(place, names):
+    barrier = pltpu.get_barrier_semaphore()
+    for name in names:
+        pl.semaphore_signal(
+            barrier, inc=1, device_id=place.device(name), device_id_type=MESH_ID
+        )
+    pl.semaphore_wait(barrier, len(names))
+
+
+class Sender:
+    def __init__(self, place, send_sems, recv_sems):
+        self.place, self.send_sems, self.recv_sems, self.used = place, send_sems, recv_sems, 0
+
+    def copy(self, source, target, name):
+        slot = self.used
+        self.used += 1
+        return pltpu.make_async_remote_copy(
+            src_ref=source,
+            dst_ref=target,
+            send_sem=self.send_sems.at[slot],
+            recv_sem=self.recv_sems.at[slot],
+            device_id=self.place.device(name),
+            device_id_type=MESH_ID,
+        )
+
+
+def part_rows(tokens):
+    unit = tokens // 16
+    first = -(-unit // 3)
+    second = -(-(unit - first) // 2)
+    return (first * 16, second * 16, (unit - first - second) * 16)
+
+
+def part_starts(tokens):
+    rows = part_rows(tokens)
+    return (0, rows[0], rows[0] + rows[1])
+
+
+def spot(tokens, part, half, core, index):
+    rows, start = part_rows(tokens)[part], part_starts(tokens)[part]
+    return half * 8 * tokens + 8 * start + core * 4 * rows + index * rows
+
+
+def gather16(tokens, buffer, own, sender):
+    links, cores = [], []
+    for part, order in enumerate(ORDERS):
+        rows, start = part_rows(tokens)[part], part_starts(tokens)[part]
+        base = spot(tokens, part, 0, 0, 0)
+        mine = own.at[pl.ds(start, rows)] if own is not None else buffer.at[pl.ds(base, rows)]
+        pairs = (
+            (mine, spot(tokens, part, 0, 0, 1), rows),
+            (buffer.at[pl.ds(base, 2 * rows)], spot(tokens, part, 0, 0, 2), 2 * rows),
+            (buffer.at[pl.ds(base, 4 * rows)], spot(tokens, part, 1, 0, 0), 4 * rows),
+        )
+        links.append(
+            [
+                sender.copy(source, buffer.at[pl.ds(target, count)], order[step])
+                for step, (source, target, count) in enumerate(pairs)
+            ]
+        )
+        moves = (
+            (mine, 0, 0, rows),
+            (None, 0, 1, rows),
+            (None, 0, 2, 2 * rows),
+            (None, 1, 0, 4 * rows),
+        )
+        cores.append(
+            [
+                sender.copy(
+                    buffer.at[pl.ds(spot(tokens, part, half, 0, index), count)]
+                    if source is None
+                    else source,
+                    buffer.at[pl.ds(spot(tokens, part, half, 1, index), count)],
+                    "core",
+                )
+                for source, half, index, count in moves
+            ]
+        )
+    return links, cores
+
+
+def gather4(tokens, buffer, own, sender, place):
+    mine = pl.ds(pl.multiple_of(place.column() * tokens, tokens), tokens)
+    theirs = pl.ds(pl.multiple_of(place.column(("x",)) * tokens, tokens), tokens)
+    return (
+        sender.copy(own, buffer.at[mine], "x"),
+        sender.copy(own, buffer.at[mine], "core"),
+        sender.copy(buffer.at[theirs], buffer.at[theirs], "core"),
+    )
+
+
+def normed(values, gain):
+    factor = lax.rsqrt(jnp.mean(values * values, axis=-1, keepdims=True) + EPSILON)
+    return values * factor * gain
+
+
+def norm_back(values, gain, grad):
+    factor = lax.rsqrt(jnp.mean(values * values, axis=-1, keepdims=True) + EPSILON)
+    unit = values * factor
+    scaled = gain * grad
+    back = factor * (scaled - unit * jnp.mean(scaled * unit, axis=-1, keepdims=True))
+    return back, jnp.sum(grad * unit, axis=0, keepdims=True)
+
+
+def start_kernel(
+    input_ref, gain_ref, grad_ref, attn_ref, grad_all, own, send_sems, recv_sems, local_sems
+):
+    tokens = input_ref.shape[0]
+    place = Place()
+    enter(place, LINKS)
+    sender = Sender(place, send_sems, recv_sems)
+    links, cores = gather16(tokens, grad_all, grad_ref, sender)
+    own[...] = normed(input_ref[...].astype(F32), gain_ref[...]).astype(BF16)
+    row_copies = gather4(tokens, attn_ref, own, sender, place)
+    row_copies[0].start()
+    row_copies[1].start()
+    keep = []
+    for part in range(3):
+        links[part][0].start()
+        cores[part][0].start()
+        rows, start = part_rows(tokens)[part], part_starts(tokens)[part]
+        keep.append(
+            pltpu.make_async_copy(
+                grad_ref.at[pl.ds(start, rows)],
+                grad_all.at[pl.ds(spot(tokens, part, 0, 0, 0), rows)],
+                local_sems.at[part],
+            )
+        )
+        keep[-1].start()
+    mine = pl.ds(pl.multiple_of(place.column() * tokens, tokens), tokens)
+    own_copy = pltpu.make_async_copy(own, attn_ref.at[mine], local_sems.at[3])
+    own_copy.start()
+    for copy in keep:
+        copy.wait()
+    for step in range(3):
+        for part in range(3):
+            links[part][step].wait_recv()
+            if step < 2:
+                links[part][step + 1].start()
+            cores[part][step + 1].start()
+        if step == 0:
+            row_copies[0].wait_recv()
+            row_copies[2].start()
+    own_copy.wait()
+    row_copies[1].wait_recv()
+    row_copies[2].wait_recv()
+    for copy in row_copies:
+        copy.wait_send()
+    for part in range(3):
+        for copy in links[part]:
+            copy.wait_send()
+        for copy in cores[part]:
+            copy.wait()
+
+
+def scatter4(partial, from_core, from_x, tokens, sender, place):
+    copies = []
+    for names in (("x", "core"), ("core",)):
+        shard = pl.ds(pl.multiple_of(place.column(names) * tokens, tokens), tokens)
+        copies.append(
+            sender.copy(partial.at[shard], from_core.at[len(copies)], "core")
+        )
+    return copies
+
+
+def sum4(partial, from_core, outgoing, from_x, tokens, sender, place):
+    copies = scatter4(partial, from_core, from_x, tokens, sender, place)
+    for copy in copies:
+        copy.start()
+    far = pl.ds(pl.multiple_of(place.column(("x",)) * tokens, tokens), tokens)
+    mine = pl.ds(pl.multiple_of(place.column() * tokens, tokens), tokens)
+    copies[0].wait_recv()
+    outgoing[...] = (partial[far, :].astype(F32) + from_core[0].astype(F32)).astype(BF16)
+    along = sender.copy(outgoing, from_x, "x")
+    along.start()
+    copies[1].wait_recv()
+    near = partial[mine, :].astype(F32) + from_core[1].astype(F32)
+    along.wait_recv()
+    total = near + from_x[...].astype(F32)
+    for copy in copies:
+        copy.wait_send()
+    along.wait_send()
+    return total
+
+
+def silu_parts(gate, up, hidden_grad):
+    s = 1.0 / (1.0 + jnp.exp(-gate))
+    silu = gate * s
+    hidden = silu * up
+    gate_grad = hidden_grad * up * s * (1.0 + gate * (1.0 - s))
+    return hidden, gate_grad, hidden_grad * silu
+
+
+def ffn_kernel(
+    partial_ref,
+    input_ref,
+    gain_ref,
+    grad_all,
+    gate_w,
+    up_w,
+    down_w,
+    residual_ref,
+    ffn_all,
+    hidden_ref,
+    pair_ref,
+    rows_ref,
+    from_core,
+    outgoing,
+    from_x,
+    ffn_buf,
+    grad_buf,
+    gate_v,
+    up_v,
+    down_v,
+    send_sems,
+    recv_sems,
+    local_sems,
+):
+    tokens = input_ref.shape[0]
+    units = gate_v.shape[1]
+    place = Place()
+    columns = pl.ds(pl.multiple_of(place.quarter() * units, units), units)
+    loads = [
+        pltpu.make_async_copy(gate_w.at[:, columns], gate_v, local_sems.at[0]),
+        pltpu.make_async_copy(up_w.at[:, columns], up_v, local_sems.at[1]),
+        pltpu.make_async_copy(down_w.at[columns, :], down_v, local_sems.at[2]),
+        pltpu.make_async_copy(grad_all, grad_buf, local_sems.at[3]),
+    ]
+    enter(place, LINKS)
+    for copy in loads:
+        copy.start()
+    sender = Sender(place, send_sems, recv_sems)
+    residual = input_ref[...].astype(F32) + sum4(
+        partial_ref, from_core, outgoing, from_x, tokens, sender, place
+    )
+    residual_ref[...] = residual
+    own = normed(residual, gain_ref[...]).astype(BF16)
+    for part in range(3):
+        rows, start = part_rows(tokens)[part], part_starts(tokens)[part]
+        ffn_buf[pl.ds(spot(tokens, part, 0, 0, 0), rows), :] = own[start : start + rows]
+    links, cores = gather16(tokens, ffn_buf, None, sender)
+    for part in range(3):
+        links[part][0].start()
+        cores[part][0].start()
+    for copy in loads:
+        copy.wait()
+    for step in range(2):
+        for part in range(3):
+            links[part][step].wait_recv()
+            links[part][step + 1].start()
+            cores[part][step + 1].start()
+    for part in range(3):
+        for copy in cores[part][:3]:
+            copy.wait_recv()
+
+    block = 2 * tokens
+
+    def compute(index):
+        rows = pl.ds(pl.multiple_of(index * block, block), block)
+        values = ffn_buf[rows, :]
+        gate = jnp.dot(values, gate_v[...], preferred_element_type=F32)
+        up = jnp.dot(values, up_v[...], preferred_element_type=F32)
+        hidden_grad = matmul_nt(grad_buf[rows, :], down_v[...])
+        hidden, gate_grad, up_grad = silu_parts(gate, up, hidden_grad)
+        hidden_ref[rows, :] = hidden.astype(BF16)
+        pair_ref[rows, :units] = gate_grad.astype(BF16)
+        pair_ref[rows, units:] = up_grad.astype(BF16)
+
+    half = 8 * tokens
+    first = pltpu.make_async_copy(
+        ffn_buf.at[pl.ds(0, half)], ffn_all.at[pl.ds(0, half)], local_sems.at[4]
+    )
+    second = pltpu.make_async_copy(
+        ffn_buf.at[pl.ds(half, half)], ffn_all.at[pl.ds(half, half)], local_sems.at[5]
+    )
+    first.start()
+    pl.loop(0, 4)(compute)
+    for part in range(3):
+        links[part][2].wait_recv()
+        cores[part][3].start()
+    for part in range(3):
+        cores[part][3].wait_recv()
+    second.start()
+    pl.loop(4, 8)(compute)
+    for part, order in enumerate(ORDERS):
+        rows, start = part_rows(tokens)[part], part_starts(tokens)[part]
+        for half_bit in range(2):
+            for core in range(2):
+                for index in range(4):
+                    bits = (index % 2, index // 2, half_bit)
+                    flips = tuple(name for name, bit in zip(order, bits) if bit)
+                    row = ("z" in flips) * 2 + ("y" in flips)
+                    names = tuple(n for n in flips if n == "x") + (("core",) if core else ())
+                    target = row * 4 * tokens + place.column(names) * tokens + start
+                    rows_ref[pl.ds(pl.multiple_of(target, 16), rows), :] = hidden_ref[
+                        pl.ds(spot(tokens, part, half_bit, core, index), rows), :
+                    ]
+    first.wait()
+    second.wait()
+    for part in range(3):
+        for copy in links[part] + cores[part]:
+            copy.wait_send()
+
+
+def back_kernel(
+    pair_ref,
+    gate_w,
+    up_w,
+    residual_ref,
+    gain_ref,
+    grad_ref,
+    back_ref,
+    gain_back_ref,
+    low_all,
+    weights,
+    products,
+    from_core,
+    third,
+    second,
+    first,
+    own,
+    send_sems,
+    recv_sems,
+    local_sems,
+):
+    tokens = residual_ref.shape[0]
+    units = pair_ref.shape[1] // 2
+    place = Place()
+    columns = pl.ds(pl.multiple_of(place.quarter() * units, units), units)
+    loads = [
+        pltpu.make_async_copy(
+            gate_w.at[:, columns], weights.at[:, pl.ds(0, units)], local_sems.at[0]
+        ),
+        pltpu.make_async_copy(
+            up_w.at[:, columns], weights.at[:, pl.ds(units, units)], local_sems.at[1]
+        ),
+    ]
+    enter(place, LINKS)
+    for copy in loads:
+        copy.start()
+    sender = Sender(place, send_sems, recv_sems)
+    part_list = [
+        (part, part_rows(tokens)[part], part_starts(tokens)[part]) for part in range(3)
+    ]
+
+    def place_of(part, half, core, index, count):
+        return pl.ds(spot(tokens, part, half, core, index), count)
+
+    to_core = [
+        [
+            sender.copy(
+                products.at[place_of(part, half, 1, 0, 4 * rows)],
+                from_core.at[pl.ds(half * 4 * tokens + 4 * start, 4 * rows)],
+                "core",
+            )
+            for part, rows, start in part_list
+        ]
+        for half in range(2)
+    ]
+    far = [
+        sender.copy(
+            products.at[place_of(part, 1, 0, 0, 4 * rows)],
+            third.at[pl.ds(4 * start, 4 * rows)],
+            ORDERS[part][2],
+        )
+        for part, rows, start in part_list
+    ]
+    middle = [
+        sender.copy(
+            products.at[place_of(part, 0, 0, 2, 2 * rows)],
+            second.at[pl.ds(2 * start, 2 * rows)],
+            ORDERS[part][1],
+        )
+        for part, rows, start in part_list
+    ]
+    close = [
+        sender.copy(
+            products.at[place_of(part, 0, 0, 1, rows)],
+            first.at[pl.ds(start, rows)],
+            ORDERS[part][0],
+        )
+        for part, rows, start in part_list
+    ]
+    for copy in loads:
+        copy.wait()
+    block = 2 * tokens
+
+    def compute(index):
+        rows = pl.ds(pl.multiple_of(index * block, block), block)
+        products[rows, :] = matmul_nt(pair_ref[rows, :], weights[...]).astype(BF16)
+
+    def add_in(rows, arrived):
+        products[rows, :] = (
+            products[rows, :].astype(F32) + arrived.astype(F32)
+        ).astype(BF16)
+
+    pl.loop(4, 8)(compute)
+    for copy in to_core[1]:
+        copy.start()
+    pl.loop(0, 2)(compute)
+    for part, rows, start in part_list:
+        to_core[1][part].wait_recv()
+        add_in(
+            place_of(part, 1, 0, 0, 4 * rows),
+            from_core[pl.ds(4 * tokens + 4 * start, 4 * rows), :],
+        )
+        far[part].start()
+    pl.loop(2, 4)(compute)
+    for copy in to_core[0]:
+        copy.start()
+    for part, rows, start in part_list:
+        to_core[0][part].wait_recv()
+        add_in(
+            place_of(part, 0, 0, 0, 4 * rows), from_core[pl.ds(4 * start, 4 * rows), :]
+        )
+    for part, rows, start in part_list:
+        far[part].wait_recv()
+        add_in(
+            place_of(part, 0, 0, 2, 2 * rows),
+            third[pl.ds(4 * start + 2 * rows, 2 * rows), :],
+        )
+        middle[part].start()
+        add_in(place_of(part, 0, 0, 0, 2 * rows), third[pl.ds(4 * start, 2 * rows), :])
+    for part, rows, start in part_list:
+        middle[part].wait_recv()
+        add_in(place_of(part, 0, 0, 1, rows), second[pl.ds(2 * start + rows, rows), :])
+        close[part].start()
+        add_in(place_of(part, 0, 0, 0, rows), second[pl.ds(2 * start, rows), :])
+    gain_total = jnp.zeros(gain_ref.shape, F32)
+    for part, rows, start in part_list:
+        close[part].wait_recv()
+        mine = pl.ds(start, rows)
+        ffn_in_grad = products[place_of(part, 0, 0, 0, rows), :].astype(F32) + first[
+            mine, :
+        ].astype(F32)
+        back, gain_part = norm_back(residual_ref[mine, :], gain_ref[...], ffn_in_grad)
+        back = back + grad_ref[mine, :].astype(F32)
+        back_ref[mine, :] = back
+        own[mine, :] = back.astype(BF16)
+        gain_total = gain_total + gain_part
+    gain_back_ref[...] = gain_total
+    row_copies = gather4(tokens, low_all, own, sender, place)
+    row_copies[0].start()
+    row_copies[1].start()
+    mine = pl.ds(pl.multiple_of(place.column() * tokens, tokens), tokens)
+    own_copy = pltpu.make_async_copy(own, low_all.at[mine], local_sems.at[2])
+    own_copy.start()
+    for copy in to_core[0] + to_core[1] + far + middle + close:
+        copy.wait_send()
+    row_copies[0].wait_recv()
+    row_copies[2].start()
+    own_copy.wait()
+    row_copies[1].wait_recv()
+    row_copies[2].wait_recv()
+    for copy in row_copies:
+        copy.wait_send()
+
+
+def end_kernel(
+    partial_ref,
+    input_ref,
+    gain_ref,
+    back_ref,
+    grad_ref,
+    gain_back_ref,
+    from_core,
+    outgoing,
+    from_x,
+    send_sems,
+    recv_sems,
+):
+    tokens = input_ref.shape[0]
+    place = Place()
+    enter(place, ("x", "core"))
+    sender = Sender(place, send_sems, recv_sems)
+    total = sum4(partial_ref, from_core, outgoing, from_x, tokens, sender, place)
+    back, gain_part = norm_back(input_ref[...].astype(F32), gain_ref[...], total)
+    grad_ref[...] = (back + back_ref[...]).astype(BF16)
+    gain_back_ref[...] = gain_part
+
+
+IN_VMEM = pl.BlockSpec(memory_space=pltpu.VMEM)
+ANYWHERE = pl.BlockSpec(memory_space=pl.ANY)
+MIB = 1 << 20
+
+
+def shape_of(shape, dtype):
+    return jax.ShapeDtypeStruct(shape, dtype)
+
+
+def call(kernel, number, ins, outs, out_specs, scratch, limit, operands, flops, moved):
+    return pl.pallas_call(
+        kernel,
+        out_shape=outs,
+        in_specs=ins,
+        out_specs=out_specs,
+        scratch_shapes=scratch,
+        cost_estimate=pl.CostEstimate(
+            flops=flops, bytes_accessed=moved, transcendentals=0
+        ),
+        compiler_params=pltpu.CompilerParams(
+            collective_id=number, has_side_effects=True, vmem_limit_bytes=limit
+        ),
+    )(*operands)
+
+
+def copies(count):
+    return [pltpu.SemaphoreType.DMA((count,)), pltpu.SemaphoreType.DMA((count,))]
+
+
+def start_step(layer_input, gain_attn, out_grad):
+    tokens, width = layer_input.shape
+    return call(
+        start_kernel,
+        0,
+        [IN_VMEM, IN_VMEM, ANYWHERE],
+        [shape_of((4 * tokens, width), BF16), shape_of((16 * tokens, width), BF16)],
+        [ANYWHERE, ANYWHERE],
+        [pltpu.VMEM((tokens, width), BF16)] + copies(24) + [pltpu.SemaphoreType.DMA((4,))],
+        32 * MIB,
+        (layer_input, gain_attn[None, :], out_grad),
+        10**6,
+        100 * 10**6,
+    )
+
+
+def ffn_step(partial, layer_input, gain_ffn, grad_all, w_gate, w_up, w_down):
+    tokens, width = layer_input.shape
+    units = w_gate.shape[1] // 4
+    everyone = 16 * tokens
+    return call(
+        ffn_kernel,
+        1,
+        [IN_VMEM, IN_VMEM, IN_VMEM, ANYWHERE, ANYWHERE, ANYWHERE, ANYWHERE],
+        [
+            shape_of((tokens, width), F32),
+            shape_of((everyone, width), BF16),
+            shape_of((everyone, units), BF16),
+            shape_of((everyone, 2 * units), BF16),
+            shape_of((everyone, units), BF16),
+        ],
+        [IN_VMEM, ANYWHERE, IN_VMEM, IN_VMEM, IN_VMEM],
+        [
+            pltpu.VMEM((2, tokens, width), BF16),
+            pltpu.VMEM((tokens, width), BF16),
+            pltpu.VMEM((tokens, width), BF16),
+            pltpu.VMEM((everyone, width), BF16),
+            pltpu.VMEM((everyone, width), BF16),
+            pltpu.VMEM((width, units), BF16),
+            pltpu.VMEM((width, units), BF16),
+            pltpu.VMEM((units, width), BF16),
+        ]
+        + copies(24)
+        + [pltpu.SemaphoreType.DMA((6,))],
+        56 * MIB,
+        (partial, layer_input, gain_ffn[None, :], grad_all, w_gate, w_up, w_down),
+        6 * everyone * width * units,
+        150 * 10**6,
+    )
+
+
+def back_step(pair, w_gate, w_up, residual, gain_ffn, out_grad):
+    tokens, width = residual.shape
+    units = pair.shape[1] // 2
+    everyone = 16 * tokens
+    return call(
+        back_kernel,
+        2,
+        [IN_VMEM, ANYWHERE, ANYWHERE, IN_VMEM, IN_VMEM, IN_VMEM],
+        [
+            shape_of((tokens, width), F32),
+            shape_of((1, width), F32),
+            shape_of((4 * tokens, width), BF16),
+        ],
+        [IN_VMEM, IN_VMEM, ANYWHERE],
+        [
+            pltpu.VMEM((width, 2 * units), BF16),
+            pltpu.VMEM((everyone, width), BF16),
+            pltpu.VMEM((everyone // 2, width), BF16),
+            pltpu.VMEM((everyone // 4, width), BF16),
+            pltpu.VMEM((everyone // 8, width), BF16),
+            pltpu.VMEM((everyone // 16, width), BF16),
+            pltpu.VMEM((tokens, width), BF16),
+        ]
+        + copies(18)
+        + [pltpu.SemaphoreType.DMA((3,))],
+        56 * MIB,
+        (pair, w_gate, w_up, residual, gain_ffn[None, :], out_grad),
+        4 * everyone * width * units,
+        150 * 10**6,
+    )
+
+
+def end_step(partial, layer_input, gain_attn, back):
+    tokens, width = layer_input.shape
+    return call(
+        end_kernel,
+        3,
+        [IN_VMEM] * 4,
+        [shape_of((tokens, width), BF16), shape_of((1, width), F32)],
+        [IN_VMEM] * 2,
+        [
+            pltpu.VMEM((2, tokens, width), BF16),
+            pltpu.VMEM((tokens, width), BF16),
+            pltpu.VMEM((tokens, width), BF16),
+        ]
+        + copies(3),
+        32 * MIB,
+        (partial, layer_input, gain_attn[None, :], back),
+        10**6,
+        50 * 10**6,
+    )
+
+
+def across(array, offset):
+    return lax.ppermute(array, "dp", [(row, row ^ offset) for row in range(8)])
+
+
+def spread(total, own_quarter, dim):
+    mine = lax.dynamic_index_in_dim(total, own_quarter, 0, keepdims=False)
+    low = total.astype(BF16)
+    blocks = [mine] + [
+        across(
+            lax.dynamic_index_in_dim(low, own_quarter ^ offset, 0, keepdims=False), offset
+        ).astype(F32)
+        for offset in range(1, 4)
+    ]
+    width = mine.shape[dim]
+    shape = list(mine.shape)
+    shape[dim] = 4 * width
+    result = jnp.zeros(shape, F32)
+    for offset, block in enumerate(blocks):
+        result = lax.dynamic_update_slice_in_dim(
+            result, block, (own_quarter ^ offset) * width, dim
+        )
+    return result
+
+
+def per_device_sixteen(
+    layer_input,
+    doc_lengths,
+    w_query,
+    w_key,
+    w_value,
+    w_out,
+    w_gate,
+    w_up,
+    w_down,
+    gain_attn,
+    gain_ffn,
+    gain_query,
+    gain_key,
+    out_grad,
+):
+    row = lax.axis_index("dp")
+    half, quarter = row // 4, row % 4
+    length = layer_input.shape[0] * 4
+    attn_in, grad_all = start_step(layer_input, gain_attn, out_grad)
+    attn_mixed, saved = attention_forward(
+        attn_in, doc_lengths, w_query, w_key, w_value, gain_query, gain_key
+    )
+    partial = jnp.dot(attn_mixed, w_out, preferred_element_type=F32).astype(BF16)
+    residual, ffn_all, hidden, pair, hidden_rows = ffn_step(
+        partial, layer_input, gain_ffn, grad_all, w_gate, w_up, w_down
+    )
+    width = ffn_all.shape[1]
+    units = hidden.shape[1]
+
+    def half_of(array, which):
+        return lax.dynamic_slice_in_dim(array, which * (width // 2), width // 2, 1)
+
+    down_sent = matmul_tn(hidden, half_of(grad_all, 1 - half)).astype(BF16)
+    pair_sent = matmul_tn(half_of(ffn_all, 1 - half), pair).astype(BF16)
+    down_came = across(down_sent, 4)
+    pair_came = across(pair_sent, 4)
+    pair, down_sent, pair_sent = lax.optimization_barrier((pair, down_sent, pair_sent))
+    residual_grad, gain_ffn_part, res_low = back_step(
+        pair, w_gate, w_up, residual, gain_ffn, out_grad
+    )
+    rows = hidden_rows.reshape(4, length, units)
+    arrived = jnp.stack([rows[0]] + [across(rows[offset], offset) for offset in range(1, 4)])
+    row_hidden = jnp.concatenate(
+        [
+            lax.dynamic_index_in_dim(arrived, quarter ^ place, 0, keepdims=False)
+            for place in range(4)
+        ],
+        axis=1,
+    )
+    layer_out = (
+        residual
+        + lax.psum_scatter(
+            jnp.dot(row_hidden, w_down, preferred_element_type=F32).astype(BF16),
+            "tensor",
+            scatter_dimension=0,
+            tiled=True,
+        ).astype(F32)
+    ).astype(BF16)
+    mixed_grad = matmul_nt(res_low, w_out).astype(BF16)
+    grad_out = line_reduce(pair_sum(attn_mixed, res_low, 1), 1)
+    query_low, key_low, value_low, gain_query_part, gain_key_part = attention_backward(
+        mixed_grad, saved, gain_query, gain_key
+    )
+    partial_in = (
+        matmul_nt(query_low, w_query) + matmul_nt(key_low, w_key) + matmul_nt(value_low, w_value)
+    ).astype(BF16)
+    input_grad, gain_attn_part = end_step(partial_in, layer_input, gain_attn, residual_grad)
+    query_cols, key_cols = query_low.shape[1], key_low.shape[1]
+    grad_qkv = line_reduce(
+        pair_sum(attn_in, jnp.concatenate([query_low, key_low, value_low], axis=1), 0), 0
+    )
+    down_total = matmul_tn(hidden, half_of(grad_all, half)) + down_came.astype(F32)
+    pair_total = matmul_tn(half_of(ffn_all, half), pair) + pair_came.astype(F32)
+    block = width // 8
+    grad_down = spread(down_total.reshape(units, 4, block).transpose(1, 0, 2), quarter, 0)
+    pair_blocks = spread_pair(pair_total.reshape(4, block, 2, units), quarter)
+    gain_sums = lax.psum(
+        (gain_attn_part[0], gain_ffn_part[0], gain_query_part, gain_key_part),
+        ("dp", "tensor"),
+    )
+    return (
+        layer_out,
+        input_grad,
+        grad_qkv[:, :query_cols],
+        grad_qkv[:, query_cols : query_cols + key_cols],
+        grad_qkv[:, query_cols + key_cols :],
+        grad_out,
+        pair_blocks[0],
+        pair_blocks[1],
+        grad_down,
+        gain_sums[0],
+        gain_sums[1],
+        gain_sums[2],
+        gain_sums[3],
+    )
+
+
+def spread_pair(total, own_quarter):
+    mine = lax.dynamic_index_in_dim(total, own_quarter, 0, keepdims=False)
+    low = total.astype(BF16)
+    blocks = [mine] + [
+        across(
+            lax.dynamic_index_in_dim(low, own_quarter ^ offset, 0, keepdims=False), offset
+        ).astype(F32)
+        for offset in range(1, 4)
+    ]
+    block, units = mine.shape[0], mine.shape[2]
+    results = []
+    for which in range(2):
+        result = jnp.zeros((block, 4 * units), F32)
+        for offset, values in enumerate(blocks):
+            result = lax.dynamic_update_slice_in_dim(
+                result, values[:, which], (own_quarter ^ offset) * units, 1
+            )
+        results.append(result)
+    return results
+
+
 def solution(mesh):
     in_specs = (
         P(("dp", "tensor"), None),
@@ -329,6 +1357,7 @@
         P(),
         P(),
     )
+    sixteen = mesh.shape["dp"] == 8 and mesh.shape["tensor"] == 4
     return jax.shard_map(
-        per_device, mesh=mesh, in_specs=in_specs, out_specs=out_specs, check_vma=False
-    )
+        per_device_sixteen if sixteen else per_device, mesh=mesh, in_specs=in_specs, out_specs=out_specs, check_vma=False
+    )

time: 1050 us -> 623 us (0.59)
  waiting for transfers between devices: 795 us -> 63.2 us
  Pallas kernels: 0 us -> 293 us
  matrix products: 139 us -> 82.4 us
  local copies, waits for them, and re-layouts: 4.31 us -> 49.6 us
  starting transfers between devices: 2.05 us -> 40.1 us
  other arithmetic: 44.3 us -> 26.4 us
    reduce_scatter x11 -> x1, waiting for transfers between devices: 726 us -> 0.01 us  [per_device_sixteen(): lax.psum_scatter(jnp.dot(row_hidden, w_down, preferred_element_type=F32)....]
    pallas_call x0 -> x4, Pallas kernels: none -> 293 us  [call(): pl.pallas_call(kernel, out_shape=outs, in_specs=ins, out_specs=out_specs,...]
    all_gather x4 -> x0, waiting for transfers between devices: 68.4 us -> none  [the longest x1 22.7 us: per_device(): lax.all_gather(residual_grad.astype(jnp.bfloat16), 'tensor', axis=0, tile...]
    ppermute x0 -> x25, waiting for transfers between devices: none -> 63.2 us  [the longest x11 34.1 us: across(): return lax.ppermute(array, 'dp', [(row, row ^ offset) for row in range(8)])]
    ppermute x0 -> x25, starting transfers between devices: none -> 40 us  [the longest x12 26.6 us: chain(): arrived = lax.ppermute(send, 'dp', pairs)]
    dot_general x7 -> x4, matrix products: 40.1 us -> 13.5 us  [matmul_nt(): lax.dot_general(left_mat, right_mat, (((1,), (1,)), ((), ())), preferred_...]
    dot_general x11 -> x9, matrix products: 40.3 us -> 20.4 us  [the longest x1 9.07 us: per_device_sixteen(): jnp.dot(row_hidden, w_down, preferred_element_type=F32).astype(BF16)]
    reshape x0 -> x3, local copies, waits for them, and re-layouts: none -> 11.6 us  [the longest x1 6.56 us: per_device_sixteen(): pair_blocks = spread_pair(pair_total.reshape(4, block, 2, units), quarter)]
  transfers between devices with their start and end apart: 15 -> 26, of which waited for: 13 -> 7; matrix products, arithmetic and copies ran while one was open for 10% -> 21% of each run, Pallas kernels for 0% -> 29%
where the time goes in v1:
time: 623 us; the launch traced here: 613 us
  Pallas kernels  293 us (47%)
  matrix products  82.4 us (13%)
  waiting for transfers between devices  63.2 us (10%)
  local copies, waits for them, and re-layouts  49.6 us (8%)
  blocking collectives  42.3 us (7%)
  starting transfers between devices  40.1 us (6%)
  other arithmetic  26.4 us (4%)
  between operations  15.9 us (3%)
    pallas_call x4, Pallas kernels, call(): pl.pallas_call(kernel, out_shape=outs, in_specs=ins, out_specs=out_specs,...  293 us
    psum x1, blocking collectives, per_device_sixteen(): lax.psum((gain_attn_part[0], gain_ffn_part[0], gain_query_part, gain_key_...  42.3 us
    ppermute x11, waiting for transfers between devices, across(): return lax.ppermute(array, 'dp', [(row, row ^ offset) for row in range(8)])  34.1 us
    dot_general x6, matrix products, matmul_tn(): lax.dot_general(left_mat, right_mat, (((0,), (0,)), ((), ())), preferred_...  33.9 us
    ppermute x12, waiting for transfers between devices, chain(): arrived = lax.ppermute(send, 'dp', pairs)  28.9 us
    ppermute x12, starting transfers between devices, chain(): arrived = lax.ppermute(send, 'dp', pairs)  26.6 us
    dot_general x4, matrix products, matmul_nt(): lax.dot_general(left_mat, right_mat, (((1,), (1,)), ((), ())), preferred_...  13.5 us
    unnamed x116, local copies, waits for them, and re-layouts  12.7 us
  transfers between devices with their start and end apart: 26, of which 7 were waited for; matrix products, arithmetic and copies ran while one was open for 21% of the time, Pallas kernels for 29%

profile of v1, /device:TPU:18, one launch (start us, length us, event | category | flops | bytes accessed | tf_op | source)
XLA Modules:
  0.0 613.3 jit_solution(9216590639570359584)
XLA Ops:
  12.0 49.7 %shard_map.237 = (bf16[512,2048]{1,0:T(8,128)(2,1)S(1)}, bf16[2048,2048]{1,0:T(8,128)(2,1)S(1)}) custom-call(bf16[128,2048]{1,0:T(8,128)(2,1)S(1)} %copy-done.4, f32[1,2048]{1,0:T(1,128)S(1)} %bitcast.202, bf16[128,2048]{1,0:T(8,128)(2,1)S(1)} %copy-done.7), custom_call_target="tpu_custom_call" | custom-call | flops 1000000 | bytes 100000000 | tf_op jit(solution)/shard_map/pallas_call | solution.py:1062
  61.7 3.3 copy-done.10
  65.0 2.2 convolution_convert_fusion.6
  69.5 1.3 multiply_reduce_fusion.3
  71.4 1.8 fusion.102
  74.4 2.1 copy-done.11
  76.5 1.6 fusion.36
  78.1 2.6 convolution_convert_fusion.1.partial_ref
  80.7 64.7 %shard_map.238 = (f32[128,2048]{1,0:T(8,128)}, bf16[2048,2048]{1,0:T(8,128)(2,1)}, bf16[2048,512]{1,0:T(8,128)(2,1)}, bf16[2048,1024]{1,0:T(8,128)(2,1)}, bf16[2048,512]{1,0:T(8,128)(2,1)}) custom-call(bf16[512,2048]{1,0:T(8,128)(2,1)} %convolution_convert_fusion.1.partial_ref, bf16[128,2048]{1,0:T(8,128)(2,1)} %input_ref.5, f32[1,2048]{1,0:T(1,128)} %bitcast.246, ...), custom_call_target="tpu_custom_call" | custom-call | flops 12884901888 | bytes 150000000 | tf_op jit(solution)/shard_map/pallas_call | solution.py:1062
  145.4 2.9 slice_bitcast_fusion.8
  148.3 2.5 collective-permute-start.2
  151.8 6.3 %fusion.28 = bf16[512,1024]{1,0:T(8,128)(2,1)} fusion(bf16[2048,512]{1,0:T(8,128)(2,1)} %get-tuple-element.88, bf16[2048,2048]{1,0:T(8,128)(2,1)} %copy-done.10, s32[]{:T(128)S(6)} %select_n.148), kind=kOutput, calls=%fused_computation.41 | convolution fusion | flops 2148007936 | bytes 7340036 | tf_op jit(solution)/shard_map/dot_general | solution.py:63
  158.4 5.7 fusion.25
  164.1 2.6 collective-permute-start.17
  166.7 161.8 %shard_map.239 = (f32[128,2048]{1,0:T(8,128)}, f32[1,2048]{1,0:T(1,128)}, bf16[512,2048]{1,0:T(8,128)(2,1)}) custom-call(bf16[2048,1024]{1,0:T(8,128)(2,1)} %get-tuple-element.90.pair_ref, bf16[2048,2048]{1,0:T(8,128)(2,1)} %gate_w.3, bf16[2048,2048]{1,0:T(8,128)(2,1)} %up_w.3, f32[128,2048]{1,0:T(8,128)} %get-tuple-element.85.residual_ref, ...), custom_call_target="tpu_custom_call" | custom-call | flops 8589934592 | bytes 150000000 | tf_op jit(solution)/shard_map/pallas_call | solution.py:1062
  328.6 3.0 convolution_convert_fusion.2
  331.6 5.0 fusion.31
  336.6 2.1 multiply_reduce_fusion
  338.7 2.6 multiply_convert_fusion
  341.3 2.4 fusion.34
  343.7 1.8 fusion.35
  346.7 4.1 copy.117
  350.8 2.5 fusion.42
  355.3 3.3 fusion.103
  358.5 2.8 fusion.104
  361.3 4.5 fusion.45
  365.8 3.0 fusion.105
  368.9 4.4 add_convert_fusion.partial_ref
  375.8 17.1 %shard_map.240 = (bf16[128,2048]{1,0:T(8,128)(2,1)S(1)}, f32[1,2048]{1,0:T(1,128)S(1)}) custom-call(bf16[512,2048]{1,0:T(8,128)(2,1)S(1)} %add_convert_fusion.partial_ref, bf16[128,2048]{1,0:T(8,128)(2,1)S(1)} %copy-done.5, f32[1,2048]{1,0:T(1,128)S(1)} %bitcast.203, f32[128,2048]{1,0:T(8,128)S(1)} %copy-done.6), custom_call_target="tpu_custom_call" | custom-call | flops 1000000 | bytes 50000000 | tf_op jit(solution)/shard_map/pallas_call | solution.py:1062
  393.0 42.3 %all-reduce.4 = (f32[2048]{0:T(1024)}, f32[2048]{0:T(1024)}, f32[64]{0:T(128)}, f32[64]{0:T(128)}) all-reduce(f32[2048]{0:T(1024)S(1)} %bitcast.204, f32[2048]{0:T(1024)S(1)} %bitcast.242, f32[64]{0:T(128)S(1)} %get-tuple-element.135, f32[64]{0:T(128)S(1)} %copy-done.47), channel_id=1, replica_groups=mesh['dp'=8,'tensor'=4] {'dp','tensor'}, use_global_device_ids=true, to_apply=%region_11.12 | all-reduce | flops 4224 | bytes 33792 | tf_op jit(solution)/shard_map/psum | solution.py:1286
  435.3 3.4 dynamic-slice_convert_fusion
  438.7 1.8 constant_dynamic-slice_fusion.5
  440.5 1.9 constant_dynamic-slice_fusion.6
  444.5 1.6 pad_maximum_fusion
  446.2 9.1 %convolution_convert_fusion = bf16[512,2048]{1,0:T(8,128)(2,1)} fusion(bf16[2048,2048]{1,0:T(8,128)(2,1)} %down_w.1, bf16[512,512]{1,0:T(8,128)(2,1)S(1)} %get-tuple-element.149, bf16[512,512]{1,0:T(8,128)(2,1)S(1)} %get-tuple-element.150, bf16[512,512]{1,0:T(8,128)(2,1)S(1)} %get-tuple-element.151, bf16[512,512]{1,0:T(8,128)(2,1)S(1)} %get-tuple-element.148), kind=kOutput, calls=%fused_computation.24 | convolution fusion | flops 4304404480 | bytes 12582912 | tf_op jit(solution)/shard_map/dot_general | solution.py:1262
  455.3 6.8 %convert_add_fusion.1 = f32[512,1024]{1,0:T(8,128)} fusion(bf16[512,1024]{1,0:T(8,128)(2,1)} %collective-permute-done.21, bf16[2048,512]{1,0:T(8,128)(2,1)} %get-tuple-element.88, bf16[2048,2048]{1,0:T(8,128)(2,1)} %copy-done.10, s32[]{:T(128)S(6)} %select_n.154), kind=kOutput, calls=%fused_computation.37 | convolution fusion | flops 2148532224 | bytes 9437188 | tf_op jit(solution)/shard_map/dot_general | solution.py:63
  462.1 3.3 reshape.352
  465.4 1.7 copy.147
  467.3 1.3 collective-permute-start.22
  468.8 1.9 fusion.22
  471.5 2.3 constant_dynamic-slice_fusion
  474.0 1.6 collective-permute-start.14
  475.7 30.2 %collective-permute-done.22 = bf16[512,256]{1,0:T(8,128)(2,1)S(1)} collective-permute-done((bf16[512,256]{1,0:T(8,128)(2,1)S(1)}, bf16[512,256]{1,0:T(8,128)(2,1)S(1)}, u32[]{:S(2)}, u32[]{:S(2)}) %collective-permute-start.22) | collective-permute-done | bytes 262176 | tf_op jit(solution)/shard_map/ppermute | solution.py:1186
  507.4 6.8 %collective-permute-done.12 = bf16[512,256]{0,1:T(8,128)(2,1)S(1)} collective-permute-done((bf16[512,256]{0,1:T(8,128)(2,1)S(1)}, bf16[512,256]{0,1:T(8,128)(2,1)S(1)}, u32[]{:S(2)}, u32[]{:S(2)}) %collective-permute-start.12) | collective-permute-done | bytes 262176 | tf_op jit(solution)/shard_map/ppermute | solution.py:387
  515.0 5.1 collective-permute-start.15
  520.1 2.1 fusion.14
  523.2 2.2 collective-permute-start.13
  527.5 4.0 collective-permute-start.16
  533.7 7.6 %convert_add_fusion = f32[1024,1024]{1,0:T(8,128)} fusion(bf16[1024,1024]{1,0:T(8,128)(2,1)} %collective-permute-done.17, bf16[2048,1024]{1,0:T(8,128)(2,1)S(1)} %copy-done.52, bf16[2048,2048]{1,0:T(8,128)(2,1)S(1)} %bitcast.249, s32[]{:T(128)S(6)} %select_n.154), kind=kOutput, calls=%fused_computation.11 | convolution fusion | flops 4297064448 | bytes 14680068 | tf_op jit(solution)/shard_map/dot_general | solution.py:63
  541.3 6.6 %reshape.351 = f32[4,256,2,512]{3,2,1,0:T(2,128)} reshape(f32[1024,1024]{1,0:T(8,128)} %convert_add_fusion) | data formatting | bytes 8388608 | tf_op jit(solution)/shard_map/reshape | solution.py:1285
  547.9 3.6 convert_element_type.364
  551.5 2.0 fusion.68
  553.5 1.9 constant_dynamic-slice_fusion.1
  555.4 2.0 copy.110
  558.5 1.6 constant_dynamic-slice_fusion.4
  561.6 1.5 collective-permute-start.19
  564.3 1.3 fusion.54
  565.6 4.6 collective-permute-start.8
  570.5 1.9 collective-permute-start.6
  572.4 2.9 collective-permute-done.18
  576.6 14.8 %collective-permute-done.8 = bf16[256,768]{1,0:T(8,128)(2,1)S(1)} collective-permute-done((bf16[256,768]{1,0:T(8,128)(2,1)S(1)}, bf16[256,768]{1,0:T(8,128)(2,1)S(1)}, u32[]{:S(2)}, u32[]{:S(2)}) %collective-permute-start.8) | collective-permute-done | bytes 393248 | tf_op jit(solution)/shard_map/ppermute | solution.py:387
  591.5 1.9 collective-permute-start.9
  593.8 7.3 %collective-permute-done.9 = bf16[256,768]{1,0:T(8,128)(2,1)S(1)} collective-permute-done((bf16[256,768]{1,0:T(8,128)(2,1)S(1)}, bf16[256,768]{1,0:T(8,128)(2,1)S(1)}, u32[]{:S(2)}, u32[]{:S(2)}) %collective-permute-start.9) | collective-permute-done | bytes 393248 | tf_op jit(solution)/shard_map/ppermute | solution.py:387
  602.9 2.3 add_convert_fusion.1
  (214 shorter events, 34.8 us)
Async XLA Ops:
  7.2 62.3 %copy-start = (bf16[2048,512]{1,0:T(8,128)(2,1)S(1)}, bf16[2048,512]{1,0:T(8,128)(2,1)}, u32[]{:S(2)}) copy-start(bf16[2048,512]{1,0:T(8,128)(2,1)} %param.16) | copy-start | bytes 6291460
  7.2 595.7 %reduce-scatter.2.cloned.1.call-start = ((), (), s32[]{:S(2)}) async-start(), calls=%async_computation.1 | async-start | bytes 2621440 | tf_op jit(solution)/shard_map/reduce_scatter | solution.py:1261
  7.2 338.3 %copy-start.42 = (s32[8]{0:T(128)}, s32[8]{0:T(128)S(1)}, u32[]{:S(2)}) copy-start(s32[8]{0:T(128)S(1)} %and_select_fusion) | copy-start | bytes 100
  12.0 55.2 %copy-start.23 = (bf16[2048,128]{1,0:T(8,128)(2,1)S(1)}, bf16[2048,128]{1,0:T(8,128)(2,1)}, u32[]{:S(2)}) copy-start(bf16[2048,128]{1,0:T(8,128)(2,1)} %param.17) | copy-start | bytes 1572868
  61.7 3.3 copy-start.10
  65.0 4.5 copy-start.2
  69.5 4.9 copy-start.18
  73.2 3.3 copy-start.11
  78.1 2.6 copy-start.33
  148.3 294.2 %collective-permute-start.2 = (bf16[512,512]{1,0:T(8,128)(2,1)}, bf16[512,512]{1,0:T(8,128)(2,1)}, u32[]{:S(2)}, u32[]{:S(2)}) collective-permute-start(bf16[512,512]{1,0:T(8,128)(2,1)} %get-tuple-element.153), channel_id=1, source_target_pairs={{0,12},{4,8},{8,4},{12,0},{16,28},{20,24},{24,20},{28,16},{1,13},{... | collective-permute-start | bytes 1572872 | tf_op jit(solution)/shard_map/ppermute | solution.py:1186
  150.8 293.0 %collective-permute-start.1 = (bf16[512,512]{1,0:T(8,128)(2,1)}, bf16[512,512]{1,0:T(8,128)(2,1)}, u32[]{:S(2)}, u32[]{:S(2)}) collective-permute-start(bf16[512,512]{1,0:T(8,128)(2,1)} %get-tuple-element.154), channel_id=1, source_target_pairs={{0,8},{4,12},{8,0},{12,4},{16,24},{20,28},{24,16},{28,20},{1,9},{5... | collective-permute-start | bytes 1572872 | tf_op jit(solution)/shard_map/ppermute | solution.py:1186
  151.8 292.7 %collective-permute-start = (bf16[512,512]{1,0:T(8,128)(2,1)}, bf16[512,512]{1,0:T(8,128)(2,1)}, u32[]{:S(2)}, u32[]{:S(2)}) collective-permute-start(bf16[512,512]{1,0:T(8,128)(2,1)} %get-tuple-element.155), channel_id=1, source_target_pairs={{0,4},{4,0},{8,12},{12,8},{16,20},{20,16},{24,28},{28,24},{1,5},{5... | collective-permute-start | bytes 1572872 | tf_op jit(solution)/shard_map/ppermute | solution.py:1186
  151.8 6.6 %copy-start.50 = (bf16[2048,2048]{1,0:T(8,128)(2,1)S(1)}, bf16[2048,2048]{1,0:T(8,128)(2,1)}, u32[]{:S(2)}) copy-start(bf16[2048,2048]{1,0:T(8,128)(2,1)} %get-tuple-element.89) | copy-start | bytes 25165828
  151.8 6.6 %copy-start.51 = (bf16[2048,1024]{1,0:T(8,128)(2,1)S(1)}, bf16[2048,1024]{1,0:T(8,128)(2,1)}, u32[]{:S(2)}) copy-start(bf16[2048,1024]{1,0:T(8,128)(2,1)} %get-tuple-element.90.pair_ref) | copy-start | bytes 12582916
  158.0 297.3 %collective-permute-start.21 = (bf16[512,1024]{1,0:T(8,128)(2,1)}, bf16[512,1024]{1,0:T(8,128)(2,1)}, u32[]{:S(2)}, u32[]{:S(2)}) collective-permute-start(bf16[512,1024]{1,0:T(8,128)(2,1)} %fusion.28), channel_id=1, source_target_pairs={{0,16},{4,20},{8,24},{12,28},{16,0},{20,4},{24,8},{28,12},{1,17},{... | collective-permute-start | bytes 3145736 | tf_op jit(solution)/shard_map/ppermute | solution.py:1186
  164.1 369.5 %collective-permute-start.17 = (bf16[1024,1024]{1,0:T(8,128)(2,1)}, bf16[1024,1024]{1,0:T(8,128)(2,1)}, u32[]{:S(2)}, u32[]{:S(2)}) collective-permute-start(bf16[1024,1024]{1,0:T(8,128)(2,1)} %fusion.25), channel_id=1, source_target_pairs={{0,16},{4,20},{8,24},{12,28},{16,0},{20,4},{24,8},{28,12},{1,17},{... | collective-permute-start | bytes 6291464 | tf_op jit(solution)/shard_map/ppermute | solution.py:1186
  166.7 161.9 %copy-start.49 = (bf16[512,2048]{1,0:T(8,128)(2,1)S(1)}, bf16[512,2048]{1,0:T(8,128)(2,1)}, u32[]{:S(2)}) copy-start(bf16[512,2048]{1,0:T(8,128)(2,1)} %param.19) | copy-start | bytes 6291460
  328.6 8.0 %slice-start = ((s8[8388608]{0:T(1024)(128)(4,1)}), s8[4194304]{0:T(1024)(128)(4,1)S(1)}, s32[]{:S(2)}) async-start(s8[8388608]{0:T(1024)(128)(4,1)} %bitcast.205), calls=%async_computation.2 | async-start | bytes 8388608
  331.6 5.0 slice-start.1
  331.6 5.0 copy-start.19
  338.7 2.6 copy-start.30
  338.7 2.6 copy-start.32
  350.8 2.7 copy-start.17
  350.8 2.8 copy-start.36
  350.8 2.8 copy-start.46
  355.3 3.3 copy-start.24
  358.5 2.8 copy-start.3
  361.3 4.5 copy-start.34
  365.8 3.0 copy-start.12
  365.8 3.0 copy-start.25
  368.9 4.5 copy-start.14
  374.5 18.5 %copy-start.41 = (f32[1,2048]{1,0:T(1,128)S(1)}, f32[1,2048]{1,0:T(1,128)}, u32[]{:S(2)}) copy-start(f32[1,2048]{1,0:T(1,128)} %get-tuple-element.95) | copy-start | bytes 24580
  374.5 18.5 %copy-start.47 = (f32[64]{0:T(128)S(1)}, f32[64]{0:T(128)}, u32[]{:S(2)}) copy-start(f32[64]{0:T(128)} %get-tuple-element.137) | copy-start | bytes 772
  435.3 5.2 copy-start.13
  440.5 4.0 copy-start.28
  442.4 26.4 %collective-permute-start.10 = (bf16[512,1024]{0,1:T(8,128)(2,1)}, bf16[512,1024]{0,1:T(8,128)(2,1)}, u32[]{:S(2)}, u32[]{:S(2)}) collective-permute-start(bf16[512,1024]{0,1:T(8,128)(2,1)} %bitcast.48), channel_id=1, source_target_pairs={{0,4},{4,0},{8,12},{12,8},{16,20},{20,16},{24,28},{28,24},{1,5},{5... | collective-permute-start | bytes 3145736 | tf_op jit(solution)/shard_map/ppermute | solution.py:330
  443.7 76.4 %collective-permute-start.3 = (bf16[1024,768]{1,0:T(8,128)(2,1)}, bf16[1024,768]{1,0:T(8,128)(2,1)}, u32[]{:S(2)}, u32[]{:S(2)}) collective-permute-start(bf16[1024,768]{1,0:T(8,128)(2,1)} %bitcast.34), channel_id=1, source_target_pairs={{0,4},{4,0},{8,12},{12,8},{16,20},{20,16},{24,28},{28,24},{1,5},{5... | collective-permute-start | bytes 4718600 | tf_op jit(solution)/shard_map/ppermute | solution.py:330
  467.2 40.0 %collective-permute-start.23 = (bf16[512,256]{1,0:T(8,128)(2,1)S(1)}, bf16[512,256]{1,0:T(8,128)(2,1)S(1)}, u32[]{:S(2)}, u32[]{:S(2)}) collective-permute-start(bf16[512,256]{1,0:T(8,128)(2,1)S(1)} %get-tuple-element.165), channel_id=1, source_target_pairs={{0,8},{4,12},{8,0},{12,4},{16,24},{20,28},{24,16},{28,20},{1,9},{5... | collective-permute-start | bytes 786440 | tf_op jit(solution)/shard_map/ppermute | solution.py:1186
  467.3 38.6 %collective-permute-start.22 = (bf16[512,256]{1,0:T(8,128)(2,1)S(1)}, bf16[512,256]{1,0:T(8,128)(2,1)S(1)}, u32[]{:S(2)}, u32[]{:S(2)}) collective-permute-start(bf16[512,256]{1,0:T(8,128)(2,1)S(1)} %get-tuple-element.166), channel_id=1, source_target_pairs={{0,4},{4,0},{8,12},{12,8},{16,20},{20,16},{24,28},{28,24},{1,5},{5... | collective-permute-start | bytes 786440 | tf_op jit(solution)/shard_map/ppermute | solution.py:1186
  468.8 64.8 %slice-start.2 = ((s8[8388608]{0:T(1024)(128)(4,1)}), s8[4194304]{0:T(1024)(128)(4,1)S(1)}, s32[]{:S(2)}) async-start(s8[8388608]{0:T(1024)(128)(4,1)} %bitcast.248), calls=%async_computation.4 | async-start | bytes 8388608
  470.7 55.9 %copy-start.16 = (bf16[512,1024]{0,1:T(8,128)(2,1)}, bf16[512,1024]{0,1:T(8,128)(2,1)S(1)}, u32[]{:S(2)}) copy-start(bf16[512,1024]{0,1:T(8,128)(2,1)S(1)} %fusion.22) | copy-start | bytes 3145732
  470.8 3.2 collective-permute-start.11
  474.0 46.1 %copy-start.15 = (f32[4,1,256,768]{3,2,1,0:T(8,128)S(1)}, f32[4,1,256,768]{3,2,1,0:T(8,128)}, u32[]{:S(2)}) copy-start(f32[4,1,256,768]{3,2,1,0:T(8,128)} %constant_dynamic-slice_fusion.6) | copy-start | bytes 9437188
  474.0 33.4 %collective-permute-start.14 = (bf16[512,256]{0,1:T(8,128)(2,1)S(1)}, bf16[512,256]{0,1:T(8,128)(2,1)S(1)}, u32[]{:S(2)}, u32[]{:S(2)}) collective-permute-start(bf16[512,256]{0,1:T(8,128)(2,1)S(1)} %get-tuple-element.176), channel_id=1, source_target_pairs={{24,16},{28,20},{25,17},{29,21},{26,18},{30,22},{27,19},{31,23}} | collective-permute-start | bytes 786440 | tf_op jit(solution)/shard_map/ppermute | solution.py:387
  505.9 8.3 %collective-permute-start.12 = (bf16[512,256]{0,1:T(8,128)(2,1)S(1)}, bf16[512,256]{0,1:T(8,128)(2,1)S(1)}, u32[]{:S(2)}, u32[]{:S(2)}) collective-permute-start(bf16[512,256]{0,1:T(8,128)(2,1)S(1)} %fusion.66), channel_id=1, source_target_pairs={{0,8},{4,12},{8,16},{12,20},{1,9},{5,13},{9,17},{13,21},{2,10},{6,... | collective-permute-start | bytes 786440 | tf_op jit(solution)/shard_map/ppermute | solution.py:387
  507.2 15.9 %collective-permute-start.24 = (bf16[512,256]{1,0:T(8,128)(2,1)S(1)}, bf16[512,256]{1,0:T(8,128)(2,1)S(1)}, u32[]{:S(2)}, u32[]{:S(2)}) collective-permute-start(bf16[512,256]{1,0:T(8,128)(2,1)S(1)} %get-tuple-element.164), channel_id=1, source_target_pairs={{0,12},{4,8},{8,4},{12,0},{16,28},{20,24},{24,20},{28,16},{1,13},{... | collective-permute-start | bytes 786440 | tf_op jit(solution)/shard_map/ppermute | solution.py:1186
  507.4 26.3 %slice-start.3 = ((s8[8388608]{0:T(1024)(128)(4,1)}), s8[4194304]{0:T(1024)(128)(4,1)S(1)}, s32[]{:S(2)}) async-start(s8[8388608]{0:T(1024)(128)(4,1)} %bitcast.248), calls=%async_computation.5 | async-start | bytes 8388608
  515.0 11.7 %collective-permute-start.15 = (bf16[512,256]{0,1:T(8,128)(2,1)S(1)}, bf16[512,256]{0,1:T(8,128)(2,1)S(1)}, u32[]{:S(2)}, u32[]{:S(2)}) collective-permute-start(bf16[512,256]{0,1:T(8,128)(2,1)S(1)} %get-tuple-element.174), channel_id=1, source_target_pairs={{16,8},{20,12},{24,16},{28,20},{17,9},{21,13},{25,17},{29,21},{18,... | collective-permute-start | bytes 786440 | tf_op jit(solution)/shard_map/ppermute | solution.py:387
  522.2 11.4 %copy-start.52 = (bf16[2048,1024]{1,0:T(8,128)(2,1)S(1)}, bf16[2048,1024]{1,0:T(8,128)(2,1)}, u32[]{:S(2)}) copy-start(bf16[2048,1024]{1,0:T(8,128)(2,1)} %get-tuple-element.90.pair_ref) | copy-start | bytes 12582916
  522.3 9.2 %collective-permute-start.4 = (bf16[256,768]{1,0:T(8,128)(2,1)S(1)}, bf16[256,768]{1,0:T(8,128)(2,1)S(1)}, u32[]{:S(2)}, u32[]{:S(2)}) collective-permute-start(bf16[256,768]{1,0:T(8,128)(2,1)S(1)} %get-tuple-element.158), channel_id=1, source_target_pairs={{0,8},{4,12},{1,9},{5,13},{2,10},{6,14},{3,11},{7,15}} | collective-permute-start | bytes 1179656 | tf_op jit(solution)/shard_map/ppermute | solution.py:387
  523.2 4.3 copy-start.21
  523.2 28.3 %collective-permute-start.13 = (bf16[512,256]{0,1:T(8,128)(2,1)}, bf16[512,256]{0,1:T(8,128)(2,1)}, u32[]{:S(2)}, u32[]{:S(2)}) collective-permute-start(bf16[512,256]{0,1:T(8,128)(2,1)} %get-tuple-element.173), channel_id=1, source_target_pairs={{0,8},{4,12},{8,16},{12,20},{16,24},{20,28},{1,9},{5,13},{9,17},{1... | collective-permute-start | bytes 786440 | tf_op jit(solution)/shard_map/ppermute | solution.py:387
  525.4 38.9 %collective-permute-start.7 = (bf16[256,768]{1,0:T(8,128)(2,1)S(1)}, bf16[256,768]{1,0:T(8,128)(2,1)}, u32[]{:S(2)}, u32[]{:S(2)}) collective-permute-start(bf16[256,768]{1,0:T(8,128)(2,1)S(1)} %get-tuple-element.159), channel_id=1, source_target_pairs={{24,16},{28,20},{25,17},{29,21},{26,18},{30,22},{27,19},{31,23}} | collective-permute-start | bytes 1179656 | tf_op jit(solution)/shard_map/ppermute | solution.py:387
  527.5 24.0 %collective-permute-start.16 = (bf16[512,256]{0,1:T(8,128)(2,1)}, bf16[512,256]{0,1:T(8,128)(2,1)}, u32[]{:S(2)}, u32[]{:S(2)}) collective-permute-start(bf16[512,256]{0,1:T(8,128)(2,1)} %fusion.65), channel_id=1, source_target_pairs={{8,0},{12,4},{16,8},{20,12},{24,16},{28,20},{9,1},{13,5},{17,9},{2... | collective-permute-start | bytes 786440 | tf_op jit(solution)/shard_map/ppermute | solution.py:387
  532.3 32.0 %collective-permute-start.5 = (bf16[256,768]{1,0:T(8,128)(2,1)}, bf16[256,768]{1,0:T(8,128)(2,1)}, u32[]{:S(2)}, u32[]{:S(2)}) collective-permute-start(bf16[256,768]{1,0:T(8,128)(2,1)} %fusion.53), channel_id=1, source_target_pairs={{0,8},{4,12},{8,16},{12,20},{1,9},{5,13},{9,17},{13,21},{2,10},{6,... | collective-permute-start | bytes 1179656 | tf_op jit(solution)/shard_map/ppermute | solution.py:387
  560.5 14.9 %collective-permute-start.18 = (bf16[256,2,512]{2,0,1:T(8,128)(2,1)S(1)}, bf16[256,2,512]{2,0,1:T(8,128)(2,1)S(1)}, u32[]{:S(2)}, u32[]{:S(2)}) collective-permute-start(bf16[256,2,512]{2,0,1:T(8,128)(2,1)S(1)} %bitcast.238), channel_id=1, source_target_pairs={{0,4},{4,0},{8,12},{12,8},{16,20},{20,16},{24,28},{28,24},{1,5},{5... | collective-permute-start | bytes 1572872 | tf_op jit(solution)/shard_map/ppermute | solution.py:1186
  561.6 14.9 %collective-permute-start.19 = (bf16[256,2,512]{2,0,1:T(8,128)(2,1)S(1)}, bf16[256,2,512]{2,0,1:T(8,128)(2,1)S(1)}, u32[]{:S(2)}, u32[]{:S(2)}) collective-permute-start(bf16[256,2,512]{2,0,1:T(8,128)(2,1)S(1)} %bitcast.237), channel_id=1, source_target_pairs={{0,8},{4,12},{8,0},{12,4},{16,24},{20,28},{24,16},{28,20},{1,9},{5... | collective-permute-start | bytes 1572872 | tf_op jit(solution)/shard_map/ppermute | solution.py:1186
  563.1 30.4 %collective-permute-start.20 = (bf16[256,2,512]{2,0,1:T(8,128)(2,1)S(1)}, bf16[256,2,512]{2,0,1:T(8,128)(2,1)S(1)}, u32[]{:S(2)}, u32[]{:S(2)}) collective-permute-start(bf16[256,2,512]{2,0,1:T(8,128)(2,1)S(1)} %bitcast.236), channel_id=1, source_target_pairs={{0,12},{4,8},{8,4},{12,0},{16,28},{20,24},{24,20},{28,16},{1,13},{... | collective-permute-start | bytes 1572872 | tf_op jit(solution)/shard_map/ppermute | solution.py:1186
  565.6 25.8 %collective-permute-start.8 = (bf16[256,768]{1,0:T(8,128)(2,1)S(1)}, bf16[256,768]{1,0:T(8,128)(2,1)S(1)}, u32[]{:S(2)}, u32[]{:S(2)}) collective-permute-start(bf16[256,768]{1,0:T(8,128)(2,1)S(1)} %get-tuple-element.157), channel_id=1, source_target_pairs={{16,8},{20,12},{24,16},{28,20},{17,9},{21,13},{25,17},{29,21},{18,... | collective-permute-start | bytes 1179656 | tf_op jit(solution)/shard_map/ppermute | solution.py:387
  570.5 23.3 %collective-permute-start.6 = (bf16[256,768]{1,0:T(8,128)(2,1)S(1)}, bf16[256,768]{1,0:T(8,128)(2,1)S(1)}, u32[]{:S(2)}, u32[]{:S(2)}) collective-permute-start(bf16[256,768]{1,0:T(8,128)(2,1)S(1)} %get-tuple-element.156), channel_id=1, source_target_pairs={{0,8},{4,12},{8,16},{12,20},{16,24},{20,28},{1,9},{5,13},{9,17},{1... | collective-permute-start | bytes 1179656 | tf_op jit(solution)/shard_map/ppermute | solution.py:387
  591.5 9.7 %collective-permute-start.9 = (bf16[256,768]{1,0:T(8,128)(2,1)S(1)}, bf16[256,768]{1,0:T(8,128)(2,1)S(1)}, u32[]{:S(2)}, u32[]{:S(2)}) collective-permute-start(bf16[256,768]{1,0:T(8,128)(2,1)S(1)} %fusion.52), channel_id=1, source_target_pairs={{8,0},{12,4},{16,8},{20,12},{24,16},{28,20},{9,1},{13,5},{17,9},{2... | collective-permute-start | bytes 1179656 | tf_op jit(solution)/shard_map/ppermute | solution.py:387
  593.8 7.5 %copy-start.20 = (f32[256,2048]{1,0:T(8,128)}, f32[256,2048]{1,0:T(8,128)S(1)}, u32[]{:S(2)}) copy-start(f32[256,2048]{1,0:T(8,128)S(1)} %get-tuple-element.212) | copy-start | bytes 6291460
  593.8 8.4 %copy-start.22 = (f32[256,2048]{1,0:T(8,128)}, f32[256,2048]{1,0:T(8,128)S(1)}, u32[]{:S(2)}) copy-start(f32[256,2048]{1,0:T(8,128)S(1)} %get-tuple-element.213) | copy-start | bytes 6291460
  601.3 4.7 copy-start.1
  (19 other events, 25.6 us)
Sparse Core Ops, SparseCore 0:
  455.5 30.3 reduce-scatter.1
